TPU v7x, 32 devices: a whole 2x2x4 slice. The times are simulated.
32 devices in a mesh: clip: 2 (over x), row: 4 (over y, core), tm: 4 (over z).
Axes of the slice: x: 2, y: 2, z: 4, core: 2. Of those that a mesh axis runs over, the one named last changes fastest.
Arguments:
- frames: bfloat16 [16, 3, 16, 1024], P('clip', None, 'tm', 'row'), may hold values from -6 to 6
- keep_list: int32 [16], P('clip'), may hold values from -1 to 7, as said below
- train_slot: int32 [8], replicated, may hold values from 0 to 7, as said below
- stem_weight: bfloat16 [81, 128], replicated, may hold values from -0.625 to 0.625
- stem_gain: float32 [128], replicated, may hold values from 0.1 to 1.9
- stem_shift: float32 [128], replicated, may hold values from -3 to 3
- mixer_weight: bfloat16 [3, 3, 384, 256], replicated, may hold values from -0.109375 to 0.109375
- mixer_gain: float32 [256], replicated, may hold values from 0.1 to 1.9
- mixer_shift: float32 [256], replicated, may hold values from -3 to 3
- down_weight: bfloat16 [1024, 256], replicated, may hold values from -0.1875 to 0.1875
- down_bias: float32 [256], replicated, may hold values from -3 to 3
Outputs:
- latents: bfloat16 [8, 8, 8, 32, 256], P('clip', 'tm', 'row')
Inputs may be any that keep to these rules, and one draw needn't show every extreme that they name: `keep_list`: each encoder position 0 to 7 is named by exactly one slot, and -1 marks a dropped slot; encoder position e belongs to index e // 4 of clip. `train_slot`: A permutation; training position t belongs to index t // 4 of clip; at most 2 encoder positions of one index of clip go to one index of clip.
All inputs are finite; a program needn't handle non-finite values.
Results may differ from a plain program's by a relative error of at most 0.0053.
Values may be sent and summed in bfloat16 or wider, within the bound.
A program may use at most 64 MiB of HBM per device.

v0:
```python
import jax
import jax.numpy as jnp
from jax import lax
from jax.sharding import PartitionSpec as P

GROUPS = 32
COLS = 64


eps = 1e-06


def from_behind(shard, axis, by):
    size = lax.axis_size(axis)
    pairs = [(i, i + by) for i in range(size) if 0 <= i + by < size]
    return lax.ppermute(shard, axis, pairs)


def extended_2(cells, sides, width):
    for axis, dim in sides:
        count = lax.axis_size(axis)
        ends = count - 1
        head = lax.slice_in_dim(cells, 0, width, axis=dim)
        tail = lax.slice_in_dim(cells, cells.shape[dim] - width, cells.shape[dim], axis=dim)
        cells = jnp.concatenate(
            [
                lax.ppermute(tail, axis, [(i, (i + 1) % count) for i in range(ends)]),
                cells,
                lax.ppermute(head, axis, [((i + 1) % count, i) for i in range(ends)]),
            ],
            axis=dim,
        )
    return cells


def surround_time(volume):
    frame_n = volume.shape[1]
    earlier = from_behind(volume[:, frame_n - 2 :], "tm", 1)
    opening = jnp.broadcast_to(volume[:, :1], earlier.shape)
    earlier = jnp.where(lax.axis_index("tm") == 0, opening, earlier)
    extended = jnp.concatenate([earlier, volume], axis=1)
    extended = extended_2(extended, (("row", 2),), 1)
    return jnp.pad(extended, ((0, 0), (0, 0), (0, 0), (1, 1), (0, 0)))


def norm_silu(hidden, gain, shift):
    batch_n, cell_n, chan_n = hidden.shape
    per_group = chan_n // GROUPS
    value_sum = jnp.sum(hidden, axis=1).reshape(batch_n, GROUPS, per_group).sum(-1)
    square_sum = jnp.sum(hidden * hidden, axis=1).reshape(batch_n, GROUPS, per_group).sum(-1)
    value_sum, square_sum = lax.psum((value_sum, square_sum), ("row", "tm"))
    cell_count = cell_n * per_group * lax.axis_size("row") * lax.axis_size("tm")
    group_mean = value_sum / cell_count
    spread = square_sum / cell_count - group_mean * group_mean
    inverse = lax.rsqrt(spread + eps)
    mean_full = jnp.repeat(group_mean, per_group, axis=1)[:, None, :]
    scale_full = jnp.repeat(inverse, per_group, axis=1)[:, None, :] * gain
    return jax.nn.silu((hidden - mean_full) * scale_full + shift)


def encode(clips, params, col_n, surround):
    (
        stem_weight,
        stem_gain,
        stem_shift,
        mixer_weight,
        mixer_gain,
        mixer_shift,
        down_weight,
        down_bias,
    ) = params
    batch_n, chan_in, frame_n, row_cells = clips.shape
    row_n = row_cells // col_n
    cell_n = frame_n * row_n * col_n
    volume = clips.reshape(batch_n, chan_in, frame_n, row_n, col_n).transpose(0, 2, 3, 4, 1)
    padded = surround(volume)
    tap_views = []
    for time_tap in range(3):
        for row_tap in range(3):
            for col_tap in range(3):
                tap_views.append(
                    padded[
                        :,
                        time_tap : time_tap + frame_n,
                        row_tap : row_tap + row_n,
                        col_tap : col_tap + col_n,
                    ]
                )
    patches = jnp.concatenate(tap_views, axis=-1).reshape(batch_n * cell_n, 27 * chan_in)
    stem = jnp.dot(patches, stem_weight, preferred_element_type=jnp.float32).reshape(
        batch_n, cell_n, -1
    )
    hidden = norm_silu(stem, stem_gain, stem_shift).astype(jnp.bfloat16)
    padded = surround(hidden.reshape(batch_n, frame_n, row_n, col_n, -1))
    accumulated = jnp.zeros((batch_n * cell_n, mixer_weight.shape[3]), jnp.float32)
    for time_tap in range(3):
        for row_tap in range(3):
            tap_strip = jnp.concatenate(
                [
                    padded[
                        :,
                        time_tap : time_tap + frame_n,
                        row_tap : row_tap + row_n,
                        col_tap : col_tap + col_n,
                    ]
                    for col_tap in range(3)
                ],
                axis=-1,
            )
            accumulated = accumulated + jnp.dot(
                tap_strip.reshape(-1, tap_strip.shape[-1]),
                mixer_weight[time_tap, row_tap],
                preferred_element_type=jnp.float32,
            )
    activated = norm_silu(accumulated.reshape(batch_n, cell_n, -1), mixer_gain, mixer_shift).astype(
        jnp.bfloat16
    )
    activated = activated.reshape(batch_n, frame_n, row_n, col_n, -1)
    pooled = (
        (activated[:, 0::2].astype(jnp.float32) + activated[:, 1::2].astype(jnp.float32)) * 0.5
    ).astype(jnp.bfloat16)
    chan_out = pooled.shape[-1]
    blocks = (
        pooled.reshape(batch_n, frame_n // 2, row_n // 2, 2, col_n // 2, 2, chan_out)
        .transpose(0, 1, 2, 4, 3, 5, 6)
        .reshape(-1, 4 * chan_out)
    )
    latent = jnp.dot(blocks, down_weight, preferred_element_type=jnp.float32) + down_bias
    return latent.astype(jnp.bfloat16).reshape(
        batch_n, frame_n // 2, row_n // 2, col_n // 2, chan_out
    )


def encode_layout(clips, params):
    return encode(clips, params, COLS, surround_time)


def select_rows(target, items, slot_n):
    flattened = items.reshape(items.shape[0], -1)
    wanted = jnp.arange(slot_n, dtype=jnp.int32)
    picker = (wanted[:, None] == target[None, :]).astype(jnp.bfloat16)
    return jnp.dot(picker, flattened, preferred_element_type=jnp.float32).astype(jnp.bfloat16)


def combine_sources(received):
    return jnp.sum(received.astype(jnp.float32), axis=0).astype(jnp.bfloat16)


def local(
    frames,
    keep_list,
    train_slot,
    stem_weight,
    stem_gain,
    stem_shift,
    mixer_weight,
    mixer_gain,
    mixer_shift,
    down_weight,
    down_bias,
):
    params = (
        stem_weight,
        stem_gain,
        stem_shift,
        mixer_weight,
        mixer_gain,
        mixer_shift,
        down_weight,
        down_bias,
    )
    group_n = lax.axis_size("clip")
    enc_dev = train_slot.shape[0] // group_n
    slot_n = group_n * enc_dev
    safe_keep = jnp.maximum(keep_list, 0)
    composed = jnp.where(keep_list >= 0, train_slot[safe_keep], -1)
    packed = select_rows(composed, frames, slot_n).reshape((group_n, enc_dev) + frames.shape[1:])
    received = lax.all_to_all(packed, "clip", split_axis=0, concat_axis=0, tiled=True)
    return encode_layout(combine_sources(received), params)


def solution(mesh):
    return jax.shard_map(
        local,
        mesh=mesh,
        in_specs=(
            P("clip", None, "tm", "row"),
            P("clip"),
            P(),
            P(),
            P(),
            P(),
            P(),
            P(),
            P(),
            P(),
            P(),
        ),
        out_specs=P("clip", "tm", "row", None, None),
        check_vma=False,
    )
```

profile of v0, /device:TPU:0, one launch (start us, length us, event | category | flops | bytes accessed | tf_op | source)
XLA Modules:
  0.0 212.4 jit_solution(7035448346933879684)
XLA Ops:
  0.0 0.9 reshape.119
  0.9 0.7 broadcast_maximum_fusion
  1.6 1.3 gather_fusion
  2.9 0.7 compare_select_fusion
  3.7 0.6 reshape.120
  4.3 4.2 %all-to-all-start = ((bf16[2,4,3,4,256]{4,3,2,1,0:T(4,128)(2,1)}), bf16[2,4,3,4,256]{4,3,2,1,0:T(4,128)(2,1)S(1)}, u32[]{:S(2)}, u32[]{:S(2)}) async-start(bf16[2,4,3,4,256]{4,3,2,1,0:T(4,128)(2,1)} %reshape.120), calls=%async_computation | async-start | bytes 98304 | tf_op jit(solution)/shard_map/all_to_all | solution.py:178
  8.5 4.0 %all-to-all-done = bf16[2,4,3,4,256]{4,3,2,1,0:T(4,128)(2,1)S(1)} async-done(((bf16[2,4,3,4,256]{4,3,2,1,0:T(4,128)(2,1)}), bf16[2,4,3,4,256]{4,3,2,1,0:T(4,128)(2,1)S(1)}, u32[]{:S(2)}, u32[]{:S(2)}) %all-to-all-start) | async-done | bytes 49184 | tf_op jit(solution)/shard_map/all_to_all | solution.py:178
  12.7 4.0 %collective-permute-start = (bf16[4,2,4,64,3]{3,2,4,1,0:T(4,128)(2,1)S(1)}, bf16[4,2,4,64,3]{3,2,4,1,0:T(4,128)(2,1)S(1)}, u32[]{:S(2)}, u32[]{:S(2)}) collective-permute-start(bf16[4,2,4,64,3]{3,2,4,1,0:T(4,128)(2,1)S(1)} %slice.325), channel_id=1, source_target_pairs={{0,1},{1,2},{2,3},{4,5},{5,6},{6,7},{8,9},{9,10},{10,11},{12,13},{... | collective-permute-start | bytes 36872 | tf_op jit(solution)/shard_map/ppermute | solution.py:16
  16.8 1.5 collective-permute-done
  18.4 1.3 collective-permute-start.2
  19.7 3.0 %collective-permute-start.1 = (bf16[4,6,1,64,3]{3,2,4,1,0:T(2,128)(2,1)S(1)}, bf16[4,6,1,64,3]{3,2,4,1,0:T(2,128)(2,1)S(1)}, u32[]{:S(2)}, u32[]{:S(2)}) collective-permute-start(bf16[4,6,1,64,3]{3,2,4,1,0:T(2,128)(2,1)S(1)} %get-tuple-element.43), channel_id=1, source_target_pairs={{0,4},{4,8},{8,12},{1,5},{5,9},{9,13},{2,6},{6,10},{10,14},{3,7},{... | collective-permute-start | bytes 27656 | tf_op jit(solution)/shard_map/ppermute | solution.py:27
  22.7 0.8 collective-permute-done.1
  25.9 2.1 %copy.36 = bf16[4,4,4,64,81]{4,3,2,1,0:T(8,128)(2,1)} copy(bf16[4,4,4,64,81]{3,2,4,1,0:T(4,128)(2,1)S(1)} %constant_dynamic-update-slice_fusion) | data formatting | bytes 1327104 | tf_op jit(solution)/shard_map/concatenate | solution.py:89
  28.1 1.7 fusion.49
  30.2 34.9 %all-reduce.3 = (f32[4,32]{1,0:T(4,128)S(1)}, f32[4,32]{1,0:T(4,128)S(1)}) all-reduce(f32[4,32]{1,0:T(4,128)S(1)} %reduce_sum.88, f32[4,32]{1,0:T(4,128)S(1)} %reduce_sum.86), channel_id=1, replica_groups=mesh['clip'=2,'row'=4,'tm'=4] {'row','tm'}, use_global_device_ids=true, to_apply=%region_6.7 | all-reduce | flops 256 | bytes 2048 | tf_op jit(solution)/shard_map/psum | solution.py:51
  65.5 0.6 multiply_convert_fusion.1
  66.2 1.3 collective-permute-start.3
  67.6 8.5 %collective-permute-done.3 = bf16[4,2,4,64,128]{4,3,2,1,0:T(8,128)(2,1)S(1)} collective-permute-done((bf16[4,2,4,64,128]{4,3,2,1,0:T(8,128)(2,1)S(1)}, bf16[4,2,4,64,128]{4,3,2,1,0:T(8,128)(2,1)S(1)}, u32[]{:S(2)}, u32[]{:S(2)}) %collective-permute-start.3) | collective-permute-done | bytes 524320 | tf_op jit(solution)/shard_map/ppermute | solution.py:16
  76.2 1.3 collective-permute-start.5
  77.5 3.2 %collective-permute-start.4 = (bf16[4,6,1,64,128]{4,3,2,1,0:T(8,128)(2,1)S(1)}, bf16[4,6,1,64,128]{4,3,2,1,0:T(8,128)(2,1)S(1)}, u32[]{:S(2)}, u32[]{:S(2)}) collective-permute-start(bf16[4,6,1,64,128]{4,3,2,1,0:T(8,128)(2,1)S(1)} %get-tuple-element.39), channel_id=1, source_target_pairs={{0,4},{4,8},{8,12},{1,5},{5,9},{9,13},{2,6},{6,10},{10,14},{3,7},{... | collective-permute-start | bytes 1179656 | tf_op jit(solution)/shard_map/ppermute | solution.py:27
  80.8 1.1 fusion.16
  81.9 1.4 select_maximum_fusion
  83.3 6.2 %fusion.50 = (bf16[4,4,4,64,128]{4,3,2,1,0:T(8,128)(2,1)}, bf16[4,4,4,64,128]{4,3,2,1,0:T(8,128)(2,1)}, bf16[4,4,4,64,128]{4,3,2,1,0:T(8,128)(2,1)}, bf16[4,4,4,...) fusion(bf16[4,6,6,66,128]{4,3,2,1,0:T(8,128)(2,1)S(1)} %select_, ...), kind=kLoop, calls=%fused_computation.143 | loop fusion | bytes 37748736 | tf_op jit(solution)/shard_map/slice | solution.py:100
  90.0 0.9 fusion.52
  91.0 1.0 fusion.51
  92.8 1.1 pad_maximum_fusion.1
  94.3 1.2 fusion.28
  95.6 1.2 convolution_add_fusion.7
  96.8 1.1 pad_maximum_fusion.3
  97.9 1.2 convolution_add_fusion.6
  99.2 1.2 convolution_add_fusion.5
  100.7 0.5 fusion.6
  101.2 1.2 convolution_add_fusion.4
  102.5 1.3 pad_maximum_fusion.5
  103.8 1.3 convolution_add_fusion.3
  105.1 1.2 convolution_add_fusion.2
  106.6 0.5 pad_maximum_fusion.7
  107.1 0.7 copy-done.9
  108.2 1.3 convolution_add_fusion.1
  109.5 3.2 %bitcast_reduce_fusion = (f32[4,256]{1,0:T(4,128)S(1)}, f32[4,256]{1,0:T(4,128)S(1)}, f32[4096,256]{1,0:T(8,128)}) fusion(f32[4096,256]{1,0:T(8,128)S(1)} %convolution_add_fusion.1, bf16[4096,384]{1,0:T(8,128)(2,1)S(1)} %bitcast.87, bf16[3,3,384,256]{3,2,1,0:T(8,128)(2,1)S(1)} %copy-done.8), kind=kOutput, calls=%fused_computation.14 | convolution fusion | flops 809498624 | bytes 11739136 | tf_op jit(solution)/shard_map/dot_general | solution.py:110
  113.0 35.9 %all-reduce.2 = (f32[4,32]{1,0:T(4,128)S(1)}, f32[4,32]{1,0:T(4,128)S(1)}) all-reduce(f32[4,32]{1,0:T(4,128)S(1)} %reduce_sum.92, f32[4,32]{1,0:T(4,128)S(1)} %reduce_sum.90), channel_id=1, replica_groups=mesh['clip'=2,'row'=4,'tm'=4] {'row','tm'}, use_global_device_ids=true, to_apply=%region_12.13 | all-reduce | flops 256 | bytes 2048 | tf_op jit(solution)/shard_map/psum | solution.py:51
  149.3 6.2 %fusion.4 = bf16[4,4,4,64,256]{4,1,3,2,0:T(4,128)(2,1)S(1)} fusion(f32[4,4,4,64,256]{4,3,2,1,0:T(8,128)} %bitcast.86, f32[256]{0:T(256)S(1)} %copy-done.13, f32[4,256]{1,0:T(4,128)S(1)} %broadcast_multiply_fusion, f32[4,256]{1,0:T(4,128)S(1)} %sub.31), kind=kLoop, calls=%fused_computation.19 | loop fusion | flops 8388608 | bytes 6300672 | tf_op jit(solution)/shard_map/convert_element_type | solution.py:115
  155.6 25.5 %slice.321 = bf16[4,2,4,64,256]{4,1,3,2,0:T(2,128)(2,1)} slice(bf16[4,4,4,64,256]{4,1,3,2,0:T(4,128)(2,1)S(1)} %fusion.4), slice={[0:4:1], [1:4:2], [0:4:1], [0:64:1], [0:256:1]} | slice | bytes 2097152 | tf_op jit(solution)/shard_map/slice | solution.py:120
  181.0 25.4 %slice.320 = bf16[4,2,4,64,256]{4,1,3,2,0:T(2,128)(2,1)} slice(bf16[4,4,4,64,256]{4,1,3,2,0:T(4,128)(2,1)S(1)} %fusion.4), slice={[0:4:1], [0:4:2], [0:4:1], [0:64:1], [0:256:1]} | slice | bytes 2097152 | tf_op jit(solution)/shard_map/slice | solution.py:120
  206.4 3.1 %multiply_convert_fusion = bf16[4,2,4,64,256]{4,1,3,2,0:T(2,128)(2,1)S(1)} fusion(bf16[4,2,4,64,256]{4,1,3,2,0:T(2,128)(2,1)} %slice.321, bf16[4,2,4,64,256]{4,1,3,2,0:T(2,128)(2,1)} %slice.320), kind=kLoop, calls=%fused_computation.44 | loop fusion | flops 2621440 | bytes 3145728 | tf_op jit(solution)/shard_map/convert_element_type | solution.py:121
  209.6 0.9 copy.39
  210.5 0.8 reshape.138
  211.3 1.1 fusion.15
  (99 shorter events, 7.1 us)
Async XLA Ops:
  0.0 211.2 %copy-start = (bf16[1024,256]{1,0:T(8,128)(2,1)S(1)}, bf16[1024,256]{1,0:T(8,128)(2,1)}, u32[]{:S(2)}) copy-start(bf16[1024,256]{1,0:T(8,128)(2,1)} %param.20) | copy-start | bytes 1572868
  4.3 8.2 %all-to-all-start = ((bf16[2,4,3,4,256]{4,3,2,1,0:T(4,128)(2,1)}), bf16[2,4,3,4,256]{4,3,2,1,0:T(4,128)(2,1)S(1)}, u32[]{:S(2)}, u32[]{:S(2)}) async-start(bf16[2,4,3,4,256]{4,3,2,1,0:T(4,128)(2,1)} %reshape.120), calls=%async_computation | async-start | bytes 98304 | tf_op jit(solution)/shard_map/all_to_all | solution.py:178
  12.6 15.5 %copy-start.11 = (bf16[81,128]{1,0:T(8,128)(2,1)S(1)}, bf16[81,128]{1,0:T(8,128)(2,1)}, u32[]{:S(2)}) copy-start(bf16[81,128]{1,0:T(8,128)(2,1)} %param.14) | copy-start | bytes 62212
  12.7 5.5 %collective-permute-start = (bf16[4,2,4,64,3]{3,2,4,1,0:T(4,128)(2,1)S(1)}, bf16[4,2,4,64,3]{3,2,4,1,0:T(4,128)(2,1)S(1)}, u32[]{:S(2)}, u32[]{:S(2)}) collective-permute-start(bf16[4,2,4,64,3]{3,2,4,1,0:T(4,128)(2,1)S(1)} %slice.325), channel_id=1, source_target_pairs={{0,1},{1,2},{2,3},{4,5},{5,6},{6,7},{8,9},{9,10},{10,11},{12,13},{... | collective-permute-start | bytes 36872 | tf_op jit(solution)/shard_map/ppermute | solution.py:16
  18.4 4.3 %collective-permute-start.2 = (bf16[4,6,1,64,3]{3,2,4,1,0:T(2,128)(2,1)S(1)}, bf16[4,6,1,64,3]{3,2,4,1,0:T(2,128)(2,1)S(1)}, u32[]{:S(2)}, u32[]{:S(2)}) collective-permute-start(bf16[4,6,1,64,3]{3,2,4,1,0:T(2,128)(2,1)S(1)} %get-tuple-element.44), channel_id=1, source_target_pairs={{4,0},{8,4},{12,8},{5,1},{9,5},{13,9},{6,2},{10,6},{14,10},{7,3},{... | collective-permute-start | bytes 27656 | tf_op jit(solution)/shard_map/ppermute | solution.py:29
  19.7 3.9 %collective-permute-start.1 = (bf16[4,6,1,64,3]{3,2,4,1,0:T(2,128)(2,1)S(1)}, bf16[4,6,1,64,3]{3,2,4,1,0:T(2,128)(2,1)S(1)}, u32[]{:S(2)}, u32[]{:S(2)}) collective-permute-start(bf16[4,6,1,64,3]{3,2,4,1,0:T(2,128)(2,1)S(1)} %get-tuple-element.43), channel_id=1, source_target_pairs={{0,4},{4,8},{8,12},{1,5},{5,9},{9,13},{2,6},{6,10},{10,14},{3,7},{... | collective-permute-start | bytes 27656 | tf_op jit(solution)/shard_map/ppermute | solution.py:27
  25.7 39.8 %copy-start.14 = (f32[128]{0:T(128)S(1)}, f32[128]{0:T(128)}, u32[]{:S(2)}) copy-start(f32[128]{0:T(128)} %param.15) | copy-start | bytes 1540
  25.8 39.8 %copy-start.15 = (f32[128]{0:T(128)S(1)}, f32[128]{0:T(128)}, u32[]{:S(2)}) copy-start(f32[128]{0:T(128)} %param.16) | copy-start | bytes 1540
  66.2 9.9 %collective-permute-start.3 = (bf16[4,2,4,64,128]{4,3,2,1,0:T(8,128)(2,1)S(1)}, bf16[4,2,4,64,128]{4,3,2,1,0:T(8,128)(2,1)S(1)}, u32[]{:S(2)}, u32[]{:S(2)}) collective-permute-start(bf16[4,2,4,64,128]{4,3,2,1,0:T(8,128)(2,1)S(1)} %slice.357), channel_id=1, source_target_pairs={{0,1},{1,2},{2,3},{4,5},{5,6},{6,7},{8,9},{9,10},{10,11},{12,13},{... | collective-permute-start | bytes 1572872 | tf_op jit(solution)/shard_map/ppermute | solution.py:16
  76.2 5.6 %collective-permute-start.5 = (bf16[4,6,1,64,128]{4,3,2,1,0:T(8,128)(2,1)S(1)}, bf16[4,6,1,64,128]{4,3,2,1,0:T(8,128)(2,1)S(1)}, u32[]{:S(2)}, u32[]{:S(2)}) collective-permute-start(bf16[4,6,1,64,128]{4,3,2,1,0:T(8,128)(2,1)S(1)} %get-tuple-element.40), channel_id=1, source_target_pairs={{4,0},{8,4},{12,8},{5,1},{9,5},{13,9},{6,2},{10,6},{14,10},{7,3},{... | collective-permute-start | bytes 1179656 | tf_op jit(solution)/shard_map/ppermute | solution.py:29
  77.5 4.4 %collective-permute-start.4 = (bf16[4,6,1,64,128]{4,3,2,1,0:T(8,128)(2,1)S(1)}, bf16[4,6,1,64,128]{4,3,2,1,0:T(8,128)(2,1)S(1)}, u32[]{:S(2)}, u32[]{:S(2)}) collective-permute-start(bf16[4,6,1,64,128]{4,3,2,1,0:T(8,128)(2,1)S(1)} %get-tuple-element.39), channel_id=1, source_target_pairs={{0,4},{4,8},{8,12},{1,5},{5,9},{9,13},{2,6},{6,10},{10,14},{3,7},{... | collective-permute-start | bytes 1179656 | tf_op jit(solution)/shard_map/ppermute | solution.py:27
  91.0 1.2 copy-start.1
  91.0 1.5 copy-start.2
  91.0 1.8 copy-start.3
  92.8 1.5 copy-start.8
  99.1 1.3 copy-start.6
  99.2 1.5 copy-start.7
  105.1 1.3 copy-start.4
  105.1 1.5 copy-start.5
  106.6 1.2 copy-start.9
  106.6 1.5 copy-start.10
  109.4 39.9 %copy-start.12 = (f32[256]{0:T(256)S(1)}, f32[256]{0:T(256)}, u32[]{:S(2)}) copy-start(f32[256]{0:T(256)} %param.18) | copy-start | bytes 3076
  109.5 39.9 %copy-start.13 = (f32[256]{0:T(256)S(1)}, f32[256]{0:T(256)}, u32[]{:S(2)}) copy-start(f32[256]{0:T(256)} %param.19) | copy-start | bytes 3076
  206.4 4.8 %copy-start.16 = (f32[256]{0:T(256)S(1)}, f32[256]{0:T(256)}, u32[]{:S(2)}) copy-start(f32[256]{0:T(256)} %param.21) | copy-start | bytes 3076
where the time goes:
time: 215 us; the launch traced here: 212 us
  local copies, waits for them, and re-layouts  71.5 us (33%)
  blocking collectives  70.8 us (33%)
  other arithmetic  20 us (9%)
  starting transfers between devices  18.4 us (9%)
  matrix products  16.1 us (7%)
  waiting for transfers between devices  14.9 us (7%)
    psum x2, blocking collectives, norm_silu(): value_sum, square_sum = lax.psum((value_sum, square_sum), ('row', 'tm'))  70.8 us
    slice x1, local copies, waits for them, and re-layouts, encode(): activated[:, 1::2].astype(jnp.float32)  25.5 us
    slice x1, local copies, waits for them, and re-layouts, encode(): activated[:, 0::2].astype(jnp.float32)  25.4 us
    dot_general x9, matrix products, encode(): jnp.dot(tap_strip.reshape(-1, tap_strip.shape[-1]), mixer_weight[time_tap...  13.2 us
    ppermute x2, waiting for transfers between devices, from_behind(): return lax.ppermute(shard, axis, pairs)  9.99 us
    slice x3, local copies, waits for them, and re-layouts, encode(): padded[:, time_tap:time_tap + frame_n, row_tap:row_tap + row_n, col_tap:c...  8.15 us
    ppermute x2, starting transfers between devices, extended_2(): lax.ppermute(tail, axis, [(i, (i + 1) % count) for i in range(ends)])  6.27 us
    convert_element_type x1, other arithmetic, encode(): norm_silu(accumulated.reshape(batch_n, cell_n, -1), mixer_gain, mixer_shift)  6.22 us
  transfers between devices with their start and end apart: 7, of which 5 were waited for; matrix products, arithmetic and copies ran while one was open for 1% of the time, Pallas kernels for 0%

commit v1 on v0

v1 whole, which is shorter than its diff:
```python
import functools

import jax
import jax.numpy as jnp
from jax import lax
from jax.experimental import pallas as pl
from jax.experimental.pallas import tpu as pltpu
from jax.sharding import PartitionSpec as P

GROUPS = 32
COLS = 64
HALO = 2
TAPS = 3
MESH = pl.DeviceIdType.MESH
F32 = jnp.float32
BF16 = jnp.bfloat16

eps = 1e-06


def iota(shape, dim):
    return lax.broadcasted_iota(jnp.int32, shape, dim)


def quot(value, by):
    return lax.shift_right_logical(value * (65536 // by + 1), 16)


def rest(value, by):
    return value - quot(value, by) * by


def dot(left, right):
    return jnp.dot(left, right, preferred_element_type=F32)


def silu(value):
    half = value * 0.5
    return half + half * jnp.tanh(half)


def one_hot(flag):
    return jnp.where(flag, 1.0, 0.0).astype(BF16)


def kernel(
    sizes,
    frames_ref,
    keep_ref,
    train_ref,
    stem_w_ref,
    stem_gain_ref,
    stem_shift_ref,
    mixer_gain_ref,
    mixer_shift_ref,
    down_bias_ref,
    mixer_hbm,
    down_hbm,
    out_ref,
    packed,
    landed,
    stem_scr,
    hidden_scr,
    mixer_scr,
    mixer_w,
    down_w,
    sums1,
    sums2,
    load_sem,
    frame_send,
    frame_recv,
    sum_send,
    sum_recv,
):
    clip_n, row_dev, time_dev, clips, chan, frame_n, row_n, rounds = sizes
    cells = row_n * COLS
    c = lax.axis_index("clip")
    r = lax.axis_index("row")
    t = lax.axis_index("tm")
    me = r * time_dev + t
    peers = row_dev * time_dev
    per_clip = frame_n * chan
    halo_cells = HALO * COLS
    wide = cells + 2 * halo_cells
    out_cells = cells + 2 * COLS
    ext_f = frame_n + HALO
    chan_mid = stem_w_ref.shape[1]
    chan_out = mixer_w.shape[1]

    load_mixer = pltpu.make_async_copy(mixer_hbm, mixer_w, load_sem.at[0])
    load_down = pltpu.make_async_copy(down_hbm, down_w, load_sem.at[1])
    load_mixer.start()
    load_down.start()

    landed[...] = jnp.zeros_like(landed)

    barrier = pltpu.get_barrier_semaphore()
    for j in range(1, peers):
        other = lax.rem(me + j, peers)
        pl.semaphore_signal(
            barrier,
            inc=1,
            device_id={"row": other // time_dev, "tm": lax.rem(other, time_dev)},
            device_id_type=MESH,
        )
    rows_near = 1 + (r > 0).astype(jnp.int32) + (r < row_dev - 1).astype(jnp.int32)
    times_near = 1 + (t > 0).astype(jnp.int32) + (t < time_dev - 1).astype(jnp.int32)
    for k in range(1, clip_n):
        for dr in (-1, 0, 1):
            for dt in (-1, 0, 1):

                @pl.when((r + dr >= 0) & (r + dr < row_dev) & (t + dt >= 0) & (t + dt < time_dev))
                def _():
                    pl.semaphore_signal(
                        barrier,
                        inc=1,
                        device_id={"clip": lax.rem(c + k, clip_n), "row": r + dr, "tm": t + dt},
                        device_id_type=MESH,
                    )

    slot_n = keep_ref.shape[1]
    enc_n = train_ref.shape[1]
    rows_in = slot_n * per_clip
    rows_out = enc_n * per_clip
    named = one_hot(iota((enc_n, slot_n), 0) == keep_ref[...])
    spread = one_hot(quot(iota((slot_n, rows_in), 1), per_clip) == iota((slot_n, rows_in), 0))
    by_row = dot(named, spread).astype(BF16)
    wanted = one_hot(quot(iota((rows_out, enc_n), 0), per_clip) == train_ref[...])
    chosen = dot(wanted, by_row)
    row_at = rest(iota((rows_out, rows_in), 0), per_clip)
    col_at = rest(iota((rows_out, rows_in), 1), per_clip)
    same = (quot(row_at, chan) == rest(col_at, frame_n)) & (
        rest(row_at, chan) == quot(col_at, frame_n)
    )
    chosen = jnp.where(same, chosen, 0.0).astype(BF16)
    picked = dot(chosen, frames_ref[...]).astype(BF16)
    packed[...] = picked.reshape(packed.shape)

    pl.semaphore_wait(barrier, peers - 1 + (clip_n - 1) * rows_near * times_near)

    def frame_copy(k, dt, dr):
        if dr == 0:
            src, dst = pl.ds(0, cells), pl.ds(halo_cells, cells)
        elif dr == 1:
            src, dst = pl.ds(cells - halo_cells, halo_cells), pl.ds(0, halo_cells)
        else:
            src, dst = pl.ds(0, halo_cells), pl.ds(halo_cells + cells, halo_cells)
        goal = lax.rem(c + k, clip_n)
        return pltpu.make_async_remote_copy(
            src_ref=packed.at[goal, :, src],
            dst_ref=landed.at[k, dt, :, dst],
            send_sem=frame_send.at[k, dt, dr + 1],
            recv_sem=frame_recv.at[k, dt, dr + 1],
            device_id={"clip": goal, "row": r + dr, "tm": t + dt},
            device_id_type=MESH,
        )

    moves = [
        (k, dt, dr)
        for k in range(clip_n - 1, -1, -1)
        for dt in (1, 0)
        for dr in (1, -1, 0)
        if (k, dt, dr) != (0, 0, 0)
    ]

    def each_move(sign, act):
        for k, dt, dr in moves:
            rr, tt = r + sign * dr, t + sign * dt
            if dr == 0 and dt == 0:
                act(frame_copy(k, dt, dr))
                continue

            @pl.when((rr >= 0) & (rr < row_dev) & (tt >= 0) & (tt < time_dev))
            def _():
                act(frame_copy(k, dt, dr))

    each_move(1, lambda copy: copy.start())
    landed[0, 0, :, halo_cells : halo_cells + cells] = packed[c]

    frames_wide = 2 * frame_n
    lines = frames_wide * chan
    depth = 256
    stem_w = stem_w_ref[...]
    taps_n = stem_w.shape[0]
    at = iota((depth, taps_n), 0)
    shift_at = quot(at, lines)
    in_shift = rest(at, lines)
    frame_at = quot(in_shift, chan)
    chan_at = in_shift - frame_at * chan
    tap_at = iota((depth, taps_n), 1)
    columns = []
    for f in range(ext_f):
        a = frame_at - f
        index = (a * (TAPS * TAPS) + shift_at) * chan + chan_at
        ok = (a >= 0) & (a < TAPS) & (at < TAPS * TAPS * lines) & (index == tap_at)
        columns.append(dot(one_hot(ok), stem_w).astype(BF16))
    stem_big = jnp.concatenate(columns, axis=1)

    lane = iota((128, 128), 1)
    source = iota((128, 128), 0)
    in_row = lane & (COLS - 1)
    col = 2 * (in_row & (COLS // 2 - 1)) + jnp.where(in_row >= COLS // 2, 1, 0)
    tables = []
    for tap in range(TAPS):
        moved = col + (tap - 1)
        ok = (moved >= 0) & (moved < COLS) & (source == (lane - in_row) + moved)
        tables.append(one_hot(ok))
    col_table = jnp.concatenate(tables, axis=1)

    half_rows = clips * per_clip
    total_rows = 2 * half_rows
    row_at = iota((total_rows, total_rows), 0)
    clip_at = quot(row_at, lines)
    in_clip = rest(row_at, lines)
    frame_at = quot(in_clip, chan)
    chan_at = in_clip - frame_at * chan
    base = clip_at * per_clip + chan_at
    before = jnp.where(t > 0, half_rows + base + frame_at * chan, base)
    goal = jnp.where(frame_at >= frame_n, base + (frame_at - frame_n) * chan, before)
    order = one_hot(goal == iota((total_rows, total_rows), 1))

    each_move(-1, lambda copy: copy.wait_recv())

    volume = landed[0].astype(F32)
    for k in range(1, clip_n):
        volume = volume + landed[k].astype(F32)
    volume = volume.astype(BF16).reshape(total_rows, wide)
    volume = dot(order, volume).astype(BF16)
    blocks = wide // 128
    stacked = jnp.concatenate(
        [volume[:, b * 128 : (b + 1) * 128] for b in range(blocks)], axis=0
    )
    shifted = dot(stacked, col_table)
    views = []
    by_tap = []
    for tap in range(TAPS):
        by_tap.append(
            jnp.concatenate(
                [
                    shifted[b * total_rows : (b + 1) * total_rows, tap * 128 : (tap + 1) * 128]
                    for b in range(blocks)
                ],
                axis=1,
            )
        )
    for row_tap in range(TAPS):
        for tap in range(TAPS):
            if row_tap % 2:
                views.append(
                    pltpu.roll(by_tap[tap], wide - row_tap * COLS, 1)[:, :out_cells]
                )
            else:
                views.append(by_tap[tap][:, row_tap * COLS : row_tap * COLS + out_cells])
    filler = jnp.zeros((depth - TAPS * TAPS * lines, out_cells), F32)

    def sum_copy(buffer, number, index, j):
        other = lax.rem(me + j, peers)
        return pltpu.make_async_remote_copy(
            src_ref=buffer.at[index, me],
            dst_ref=buffer.at[index, me],
            send_sem=sum_send.at[number, j],
            recv_sem=sum_recv.at[number, j],
            device_id={"row": other // time_dev, "tm": lax.rem(other, time_dev)},
            device_id_type=MESH,
        )

    def send_sums(buffer, number, index):
        for j in range(1, peers):
            sum_copy(buffer, number, index, j).start()

    def take_sums(buffer, number, index, gain, shift):
        for j in range(1, peers):
            sum_copy(buffer, number, index, j).wait_recv()
        total = buffer[index, 0]
        for j in range(1, peers):
            total = total + buffer[index, j]
        chan_n = total.shape[1]
        per_group = chan_n // GROUPS
        joined = jnp.where(
            quot(iota((chan_n, chan_n), 0), per_group) == quot(iota((chan_n, chan_n), 1), per_group),
            1.0,
            0.0,
        )
        total = jnp.dot(
            total, joined, preferred_element_type=F32, precision=lax.Precision.HIGHEST
        )
        count = peers * frame_n * cells * per_group
        total = total * (1.0 / count)
        half = total.shape[0] // 2
        mean = total[:half]
        inverse = lax.rsqrt(total[half:] - mean * mean + eps)
        scale = inverse * gain
        return scale, shift - mean * scale

    per_round = clips // rounds
    for turn in range(rounds):
        for pos in range(per_round):
            k = turn * per_round + pos
            patches = jnp.concatenate(
                [view[k * lines : (k + 1) * lines] for view in views] + [filler], axis=0
            ).astype(BF16)
            stem = lax.dot_general(
                patches, stem_big, (((0,), (0,)), ((), ())), preferred_element_type=F32
            )
            stem_scr[k] = stem
            own = stem[COLS : COLS + cells, HALO * chan_mid :]
            values = jnp.sum(own, axis=0, keepdims=True)
            squares = jnp.sum(own * own, axis=0, keepdims=True)
            value_sum = values[:, :chan_mid]
            square_sum = squares[:, :chan_mid]
            for f in range(1, frame_n):
                value_sum = value_sum + values[:, f * chan_mid : (f + 1) * chan_mid]
                square_sum = square_sum + squares[:, f * chan_mid : (f + 1) * chan_mid]
            sums1[turn, me, pos : pos + 1, :] = value_sum
            sums1[turn, me, per_round + pos : per_round + pos + 1, :] = square_sum
        send_sums(sums1, turn, turn)

    top = jnp.where(r > 0, 1.0, 0.0).astype(F32)
    bottom = jnp.where(r < row_dev - 1, 1.0, 0.0).astype(F32)
    ext_rows = row_n + 2
    half_cols = COLS // 2
    x_at = iota((ext_rows * half_cols, chan_mid), 0) & (half_cols - 1)

    def norm_first(k, scale, shift):
        for f in range(ext_f):
            value = stem_scr[k, :, f * chan_mid : (f + 1) * chan_mid]
            value = silu(value * scale + shift)
            value = jnp.concatenate(
                [
                    value[:COLS] * top,
                    value[COLS : COLS + cells],
                    value[COLS + cells :] * bottom,
                ],
                axis=0,
            )
            parts = value.reshape(ext_rows, 2, half_cols, chan_mid)
            even, odd = parts[:, 0], parts[:, 1]
            flat = (ext_rows * half_cols, chan_mid)
            left = jnp.where(x_at == 0, 0.0, pltpu.roll(odd.reshape(flat), 1, 0))
            right = jnp.where(
                x_at == half_cols - 1, 0.0, pltpu.roll(even.reshape(flat), flat[0] - 1, 0)
            )
            left = left.reshape(even.shape)
            right = right.reshape(even.shape)
            before = jnp.stack([left, even], axis=1).reshape(value.shape)
            after = jnp.stack([odd, right], axis=1).reshape(value.shape)
            hidden_scr[k, f, :, :chan_mid] = before.astype(BF16)
            hidden_scr[k, f, :, chan_mid : 2 * chan_mid] = value.astype(BF16)
            hidden_scr[k, f, :, 2 * chan_mid :] = after.astype(BF16)

    def mix(k, turn, pos):
        value_sum = jnp.zeros((1, chan_out), F32)
        square_sum = jnp.zeros((1, chan_out), F32)
        for f in range(frame_n):
            strip = jnp.concatenate(
                [
                    hidden_scr[k, f + a, b * COLS : b * COLS + cells, :]
                    for a in range(TAPS)
                    for b in range(TAPS)
                ],
                axis=1,
            )
            mixed = dot(strip, mixer_w[...])
            mixer_scr[k, f] = mixed
            value_sum = value_sum + jnp.sum(mixed, axis=0, keepdims=True)
            square_sum = square_sum + jnp.sum(mixed * mixed, axis=0, keepdims=True)
        sums2[turn, me, pos : pos + 1, :] = value_sum
        sums2[turn, me, per_round + pos : per_round + pos + 1, :] = square_sum

    load_mixer.wait()
    for turn in range(rounds):
        scale, shift = take_sums(sums1, turn, turn, stem_gain_ref[...], stem_shift_ref[...])
        for pos in range(per_round):
            k = turn * per_round + pos
            norm_first(k, scale[pos : pos + 1], shift[pos : pos + 1])
            mix(k, turn, pos)
        send_sums(sums2, rounds + turn, turn)

    load_down.wait()
    bias = down_bias_ref[...]
    pairs = frame_n // 2
    out_rows = row_n // 2
    for turn in range(rounds):
        scale, shift = take_sums(
            sums2, rounds + turn, turn, mixer_gain_ref[...], mixer_shift_ref[...]
        )
        for pos in range(per_round):
            k = turn * per_round + pos
            squares = []
            for pair in range(pairs):
                acts = []
                for f in (2 * pair, 2 * pair + 1):
                    value = mixer_scr[k, f] * scale[pos : pos + 1] + shift[pos : pos + 1]
                    acts.append(silu(value).astype(BF16).astype(F32))
                pooled = ((acts[0] + acts[1]) * 0.5).astype(BF16)
                pooled = pooled.reshape(out_rows, 2, 2, half_cols, chan_out)
                squares.append(
                    jnp.concatenate(
                        [
                            pooled[:, p, q].reshape(out_rows * half_cols, chan_out)
                            for p in range(2)
                            for q in range(2)
                        ],
                        axis=1,
                    )
                )
            block = jnp.concatenate(squares, axis=0)
            latent = dot(block, down_w[...]) + bias
            size = block.shape[0]
            out_ref[k * size : (k + 1) * size, :] = latent.astype(BF16)

    each_move(1, lambda copy: copy.wait_send())
    for turn in range(rounds):
        for j in range(1, peers):
            sum_copy(sums1, turn, turn, j).wait_send()
            sum_copy(sums2, rounds + turn, turn, j).wait_send()


def local(
    frames,
    keep_list,
    train_slot,
    stem_weight,
    stem_gain,
    stem_shift,
    mixer_weight,
    mixer_gain,
    mixer_shift,
    down_weight,
    down_bias,
):
    clip_n = lax.axis_size("clip")
    row_dev = lax.axis_size("row")
    time_dev = lax.axis_size("tm")
    slots, chan, frame_n, cells = frames.shape
    clips = train_slot.shape[0] // clip_n
    row_n = cells // COLS
    chan_mid = stem_weight.shape[1]
    chan_out = mixer_weight.shape[3]
    rounds = 2 if clips % 2 == 0 else 1
    per_round = clips // rounds
    peers = row_dev * time_dev
    ext_f = frame_n + HALO
    out_cells = cells + 2 * COLS
    sizes = (clip_n, row_dev, time_dev, clips, chan, frame_n, row_n, rounds)
    out_rows = clips * (frame_n // 2) * (row_n // 2) * (COLS // 2)
    mixer_flat = mixer_weight.reshape(-1, chan_out)
    vmem = pl.BlockSpec(memory_space=pltpu.VMEM)
    hbm = pl.BlockSpec(memory_space=pl.ANY)
    out = pl.pallas_call(
        functools.partial(kernel, sizes),
        out_shape=jax.ShapeDtypeStruct((out_rows, chan_out), BF16),
        in_specs=[vmem] * 9 + [hbm] * 2,
        out_specs=vmem,
        scratch_shapes=[
            pltpu.VMEM((clip_n, clips * frame_n * chan, cells), BF16),
            pltpu.VMEM((clip_n, 2, clips * frame_n * chan, cells + 2 * HALO * COLS), BF16),
            pltpu.VMEM((clips, out_cells, ext_f * chan_mid), F32),
            pltpu.VMEM((clips, ext_f, out_cells, TAPS * chan_mid), BF16),
            pltpu.VMEM((clips, frame_n, cells, chan_out), F32),
            pltpu.VMEM(mixer_flat.shape, BF16),
            pltpu.VMEM(down_weight.shape, BF16),
            pltpu.VMEM((rounds, peers, 2 * per_round, chan_mid), F32),
            pltpu.VMEM((rounds, peers, 2 * per_round, chan_out), F32),
            pltpu.SemaphoreType.DMA((2,)),
            pltpu.SemaphoreType.DMA((clip_n, 2, 3)),
            pltpu.SemaphoreType.DMA((clip_n, 2, 3)),
            pltpu.SemaphoreType.DMA((2 * rounds, peers)),
            pltpu.SemaphoreType.DMA((2 * rounds, peers)),
        ],
        compiler_params=pltpu.CompilerParams(
            collective_id=0, has_side_effects=True, vmem_limit_bytes=50 * 1024 * 1024
        ),
    )(
        frames.reshape(slots * chan * frame_n, cells),
        keep_list[None],
        train_slot[None],
        stem_weight,
        stem_gain[None],
        stem_shift[None],
        mixer_gain[None],
        mixer_shift[None],
        down_bias[None],
        mixer_flat,
        down_weight,
    )
    return out.reshape(clips, frame_n // 2, row_n // 2, COLS // 2, chan_out)


def solution(mesh):
    return jax.shard_map(
        local,
        mesh=mesh,
        in_specs=(
            P("clip", None, "tm", "row"),
            P("clip"),
            P(),
            P(),
            P(),
            P(),
            P(),
            P(),
            P(),
            P(),
            P(),
        ),
        out_specs=P("clip", "tm", "row", None, None),
        check_vma=False,
    )
```

time: 215 us -> 40.7 us (0.19); the launches traced: 212 us -> 40.3 us
  blocking collectives: 70.8 us -> 0 us
  local copies, waits for them, and re-layouts: 71.5 us -> 9.42 us
  Pallas kernels: 0 us -> 30.9 us
  other arithmetic: 20 us -> 0 us
  starting transfers between devices: 18.4 us -> 0 us
  matrix products: 16.1 us -> 0 us
  waiting for transfers between devices: 14.9 us -> 0 us
    psum x2 -> x0, blocking collectives: 70.8 us -> none  [norm_silu(): value_sum, square_sum = lax.psum((value_sum, square_sum), ('row', 'tm'))]
    slice x7 -> x0, local copies, waits for them, and re-layouts: 59.1 us -> none  [the longest x1 25.5 us: encode(): activated[:, 1::2].astype(jnp.float32)]
    pallas_call x0 -> x1, Pallas kernels: none -> 30.9 us  [local(): pl.pallas_call(functools.partial(kernel, sizes), out_shape=jax.ShapeDtype...]
    dot_general x12 -> x0, matrix products: 16.1 us -> none  [the longest x9 13.2 us: encode(): jnp.dot(tap_strip.reshape(-1, tap_strip.shape[-1]), mixer_weight[time_tap...]
    ppermute x6 -> x0, starting transfers between devices: 14.2 us -> none  [the longest x2 6.27 us: extended_2(): lax.ppermute(tail, axis, [(i, (i + 1) % count) for i in range(ends)])]
    ppermute x6 -> x0, waiting for transfers between devices: 10.9 us -> none  [the longest x2 9.99 us: from_behind(): return lax.ppermute(shard, axis, pairs)]
    convert_element_type x3 -> x0, other arithmetic: 9.99 us -> none  [the longest x1 6.22 us: encode(): norm_silu(accumulated.reshape(batch_n, cell_n, -1), mixer_gain, mixer_shift)]
    concatenate x12 -> x0, other arithmetic: 8.09 us -> none  [the longest x5 4.47 us: encode(): jnp.concatenate([padded[:, time_tap:time_tap + frame_n, row_tap:row_tap +...]
  transfers between devices with their start and end apart: 7 -> 0, of which waited for: 5 -> 0; matrix products, arithmetic and copies ran while one was open for 1% -> 0% of each run, Pallas kernels for 0% -> 0%
where the time goes in v1:
time: 40.7 us; the launch traced here: 40.3 us
  Pallas kernels  30.9 us (76%)
  local copies, waits for them, and re-layouts  9.42 us (23%)
    pallas_call x1, Pallas kernels, local(): pl.pallas_call(functools.partial(kernel, sizes), out_shape=jax.ShapeDtype...  30.9 us
    unnamed x21, local copies, waits for them, and re-layouts  8.6 us
    reshape x1, local copies, waits for them, and re-layouts, local(): frames.reshape(slots * chan * frame_n, cells)  0.81 us

profile of v1, /device:TPU:0, one launch (start us, length us, event | category | flops | bytes accessed | tf_op | source)
XLA Modules:
  0.0 40.3 jit_solution(7382473362381261645)
XLA Ops:
  0.0 0.8 %reshape.9.frames_ref = bf16[96,256]{1,0:T(8,128)(2,1)S(1)} reshape(bf16[8,3,4,256]{3,2,1,0:T(4,128)(2,1)} %param.11) | data formatting | bytes 98304 | tf_op jit(solution)/shard_map/reshape | solution.py:475
  0.8 0.0 copy-start
  0.8 1.5 %copy-done = bf16[3,3,384,256]{3,2,1,0:T(8,128)(2,1)S(1)} copy-done((bf16[3,3,384,256]{3,2,1,0:T(8,128)(2,1)S(1)}, bf16[3,3,384,256]{3,2,1,0:T(8,128)(2,1)}, u32[]{:S(2)}) %copy-start) | copy-done | bytes 1769496
  2.3 0.0 copy-start.1
  2.3 1.0 %copy-done.1 = bf16[1024,256]{1,0:T(8,128)(2,1)S(1)} copy-done((bf16[1024,256]{1,0:T(8,128)(2,1)S(1)}, bf16[1024,256]{1,0:T(8,128)(2,1)}, u32[]{:S(2)}) %copy-start.1) | copy-done | bytes 524312
  3.3 0.0 copy-start.2
  3.3 0.7 %copy-done.2 = bf16[81,128]{1,0:T(8,128)(2,1)S(1)} copy-done((bf16[81,128]{1,0:T(8,128)(2,1)S(1)}, bf16[81,128]{1,0:T(8,128)(2,1)}, u32[]{:S(2)}) %copy-start.2) | copy-done | bytes 20760
  4.1 0.0 copy-start.3
  4.1 0.7 %copy-done.3 = f32[256]{0:T(256)S(1)} copy-done((f32[256]{0:T(256)S(1)}, f32[256]{0:T(256)}, u32[]{:S(2)}) %copy-start.3) | copy-done | bytes 1048
  4.8 0.0 copy-start.4
  4.8 0.7 %copy-done.4 = f32[256]{0:T(256)S(1)} copy-done((f32[256]{0:T(256)S(1)}, f32[256]{0:T(256)}, u32[]{:S(2)}) %copy-start.4) | copy-done | bytes 1048
  5.4 0.0 copy-start.5
  5.4 0.7 %copy-done.5 = f32[256]{0:T(256)S(1)} copy-done((f32[256]{0:T(256)S(1)}, f32[256]{0:T(256)}, u32[]{:S(2)}) %copy-start.5) | copy-done | bytes 1048
  6.1 0.0 copy-start.6
  6.1 0.7 %copy-done.6 = s32[8]{0:T(128)S(1)} copy-done((s32[8]{0:T(128)S(1)}, s32[8]{0:T(128)}, u32[]{:S(2)}) %copy-start.6) | copy-done | bytes 56
  6.8 0.0 copy-start.7
  6.8 0.7 %copy-done.7 = s32[8]{0:T(128)S(1)} copy-done((s32[8]{0:T(128)S(1)}, s32[8]{0:T(128)}, u32[]{:S(2)}) %copy-start.7) | copy-done | bytes 56
  7.4 0.0 copy-start.8
  7.4 0.7 %copy-done.8 = f32[128]{0:T(128)S(1)} copy-done((f32[128]{0:T(128)S(1)}, f32[128]{0:T(128)}, u32[]{:S(2)}) %copy-start.8) | copy-done | bytes 536
  8.1 0.0 copy-start.9
  8.1 0.7 %copy-done.9 = f32[128]{0:T(128)S(1)} copy-done((f32[128]{0:T(128)S(1)}, f32[128]{0:T(128)}, u32[]{:S(2)}) %copy-start.9) | copy-done | bytes 536
  8.7 30.9 %shard_map.109 = bf16[512,256]{1,0:T(8,128)(2,1)S(1)} custom-call(bf16[96,256]{1,0:T(8,128)(2,1)S(1)} %reshape.9.frames_ref, s32[1,8]{1,0:T(1,128)S(1)} %bitcast.14, s32[1,8]{1,0:T(1,128)S(1)} %bitcast.15, bf16[81,128]{1,0:T(8,128)(2,1)S(1)} %copy-done.2, f32[1,128]{1,0:T(1,128)S(1)} %bitcast.16, f32[1,128]{1,0:T(1,128)S(1)} %bitcast.17, ...), custom_call_target="tpu_custom_call" | custom-call | tf_op jit(solution)/shard_map/pallas_call | solution.py:450
  39.6 0.7 %copy.13 = bf16[4,2,2,32,256]{4,3,2,1,0:T(8,128)(2,1)} copy(bf16[4,2,2,32,256]{4,3,2,1,0:T(8,128)(2,1)S(1)} %bitcast.10) | data formatting | bytes 524288
Async XLA Ops:
  0.8 1.5 %copy-start = (bf16[3,3,384,256]{3,2,1,0:T(8,128)(2,1)S(1)}, bf16[3,3,384,256]{3,2,1,0:T(8,128)(2,1)}, u32[]{:S(2)}) copy-start(bf16[3,3,384,256]{3,2,1,0:T(8,128)(2,1)} %param.17) | copy-start | bytes 5308420
  2.3 1.0 %copy-start.1 = (bf16[1024,256]{1,0:T(8,128)(2,1)S(1)}, bf16[1024,256]{1,0:T(8,128)(2,1)}, u32[]{:S(2)}) copy-start(bf16[1024,256]{1,0:T(8,128)(2,1)} %down_hbm.1) | copy-start | bytes 1572868
  3.3 0.7 %copy-start.2 = (bf16[81,128]{1,0:T(8,128)(2,1)S(1)}, bf16[81,128]{1,0:T(8,128)(2,1)}, u32[]{:S(2)}) copy-start(bf16[81,128]{1,0:T(8,128)(2,1)} %stem_w_ref.1) | copy-start | bytes 62212
  4.1 0.7 %copy-start.3 = (f32[256]{0:T(256)S(1)}, f32[256]{0:T(256)}, u32[]{:S(2)}) copy-start(f32[256]{0:T(256)} %param.18) | copy-start | bytes 3076
  4.8 0.7 %copy-start.4 = (f32[256]{0:T(256)S(1)}, f32[256]{0:T(256)}, u32[]{:S(2)}) copy-start(f32[256]{0:T(256)} %param.19) | copy-start | bytes 3076
  5.4 0.7 %copy-start.5 = (f32[256]{0:T(256)S(1)}, f32[256]{0:T(256)}, u32[]{:S(2)}) copy-start(f32[256]{0:T(256)} %param.21) | copy-start | bytes 3076
  6.1 0.7 %copy-start.6 = (s32[8]{0:T(128)S(1)}, s32[8]{0:T(128)}, u32[]{:S(2)}) copy-start(s32[8]{0:T(128)} %param.12) | copy-start | bytes 100
  6.8 0.7 %copy-start.7 = (s32[8]{0:T(128)S(1)}, s32[8]{0:T(128)}, u32[]{:S(2)}) copy-start(s32[8]{0:T(128)} %param.13) | copy-start | bytes 100
  7.4 0.7 %copy-start.8 = (f32[128]{0:T(128)S(1)}, f32[128]{0:T(128)}, u32[]{:S(2)}) copy-start(f32[128]{0:T(128)} %param.15) | copy-start | bytes 1540
  8.1 0.7 %copy-start.9 = (f32[128]{0:T(128)S(1)}, f32[128]{0:T(128)}, u32[]{:S(2)}) copy-start(f32[128]{0:T(128)} %param.16) | copy-start | bytes 1540

commit v2 on v1

--- a/solution.py
+++ b/solution.py
@@ -45,25 +45,34 @@
 
 def kernel(
     sizes,
+    frames_hbm,
+    keep_hbm,
+    train_hbm,
+    stem_w_hbm,
+    stem_gain_hbm,
+    stem_shift_hbm,
+    mixer_w_hbm,
+    mixer_gain_hbm,
+    mixer_shift_hbm,
+    down_w_hbm,
+    down_bias_hbm,
+    out_ref,
     frames_ref,
     keep_ref,
     train_ref,
     stem_w_ref,
     stem_gain_ref,
     stem_shift_ref,
+    mixer_w,
     mixer_gain_ref,
     mixer_shift_ref,
+    down_w,
     down_bias_ref,
-    mixer_hbm,
-    down_hbm,
-    out_ref,
     packed,
     landed,
     stem_scr,
     hidden_scr,
     mixer_scr,
-    mixer_w,
-    down_w,
     sums1,
     sums2,
     load_sem,
@@ -87,10 +96,26 @@
     chan_mid = stem_w_ref.shape[1]
     chan_out = mixer_w.shape[1]
 
-    load_mixer = pltpu.make_async_copy(mixer_hbm, mixer_w, load_sem.at[0])
-    load_down = pltpu.make_async_copy(down_hbm, down_w, load_sem.at[1])
-    load_mixer.start()
-    load_down.start()
+    loads = [
+        pltpu.make_async_copy(source, target, load_sem.at[number])
+        for number, (source, target) in enumerate(
+            (
+                (frames_hbm, frames_ref),
+                (keep_hbm, keep_ref),
+                (train_hbm, train_ref),
+                (stem_w_hbm, stem_w_ref),
+                (stem_gain_hbm, stem_gain_ref),
+                (stem_shift_hbm, stem_shift_ref),
+                (mixer_w_hbm, mixer_w),
+                (mixer_gain_hbm, mixer_gain_ref),
+                (mixer_shift_hbm, mixer_shift_ref),
+                (down_w_hbm, down_w),
+                (down_bias_hbm, down_bias_ref),
+            )
+        )
+    ]
+    for load in loads:
+        load.start()
 
     landed[...] = jnp.zeros_like(landed)
 
@@ -117,6 +142,9 @@
                         device_id={"clip": lax.rem(c + k, clip_n), "row": r + dr, "tm": t + dt},
                         device_id_type=MESH,
                     )
+
+    for load in loads[:3]:
+        load.wait()
 
     slot_n = keep_ref.shape[1]
     enc_n = train_ref.shape[1]
@@ -133,7 +161,10 @@
         rest(row_at, chan) == quot(col_at, frame_n)
     )
     chosen = jnp.where(same, chosen, 0.0).astype(BF16)
-    picked = dot(chosen, frames_ref[...]).astype(BF16)
+    flat_frames = jnp.concatenate(
+        [frames_ref[s, i].astype(F32) for s in range(slot_n) for i in range(chan)], axis=0
+    ).astype(BF16)
+    picked = dot(chosen, flat_frames).astype(BF16)
     packed[...] = picked.reshape(packed.shape)
 
     pl.semaphore_wait(barrier, peers - 1 + (clip_n - 1) * rows_near * times_near)
@@ -180,6 +211,7 @@
     frames_wide = 2 * frame_n
     lines = frames_wide * chan
     depth = 256
+    loads[3].wait()
     stem_w = stem_w_ref[...]
     taps_n = stem_w.shape[0]
     at = iota((depth, taps_n), 0)
@@ -349,25 +381,25 @@
             hidden_scr[k, f, :, 2 * chan_mid :] = after.astype(BF16)
 
     def mix(k, turn, pos):
-        value_sum = jnp.zeros((1, chan_out), F32)
-        square_sum = jnp.zeros((1, chan_out), F32)
-        for f in range(frame_n):
-            strip = jnp.concatenate(
-                [
-                    hidden_scr[k, f + a, b * COLS : b * COLS + cells, :]
-                    for a in range(TAPS)
-                    for b in range(TAPS)
-                ],
-                axis=1,
-            )
-            mixed = dot(strip, mixer_w[...])
-            mixer_scr[k, f] = mixed
-            value_sum = value_sum + jnp.sum(mixed, axis=0, keepdims=True)
-            square_sum = square_sum + jnp.sum(mixed * mixed, axis=0, keepdims=True)
+        strip = jnp.concatenate(
+            [
+                hidden_scr[k, a : a + frame_n, b * COLS : b * COLS + cells, :].reshape(
+                    frame_n * cells, TAPS * chan_mid
+                )
+                for a in range(TAPS)
+                for b in range(TAPS)
+            ],
+            axis=1,
+        )
+        mixed = dot(strip, mixer_w[...])
+        mixer_scr[k] = mixed.reshape(frame_n, cells, chan_out)
+        value_sum = jnp.sum(mixed, axis=0, keepdims=True)
+        square_sum = jnp.sum(mixed * mixed, axis=0, keepdims=True)
         sums2[turn, me, pos : pos + 1, :] = value_sum
         sums2[turn, me, per_round + pos : per_round + pos + 1, :] = square_sum
 
-    load_mixer.wait()
+    for load in loads[4:7]:
+        load.wait()
     for turn in range(rounds):
         scale, shift = take_sums(sums1, turn, turn, stem_gain_ref[...], stem_shift_ref[...])
         for pos in range(per_round):
@@ -376,7 +408,8 @@
             mix(k, turn, pos)
         send_sums(sums2, rounds + turn, turn)
 
-    load_down.wait()
+    for load in loads[7:]:
+        load.wait()
     bias = down_bias_ref[...]
     pairs = frame_n // 2
     out_rows = row_n // 2
@@ -444,46 +477,45 @@
     out_cells = cells + 2 * COLS
     sizes = (clip_n, row_dev, time_dev, clips, chan, frame_n, row_n, rounds)
     out_rows = clips * (frame_n // 2) * (row_n // 2) * (COLS // 2)
-    mixer_flat = mixer_weight.reshape(-1, chan_out)
+    operands = (
+        frames,
+        keep_list[None],
+        train_slot[None],
+        stem_weight,
+        stem_gain[None],
+        stem_shift[None],
+        mixer_weight.reshape(-1, chan_out),
+        mixer_gain[None],
+        mixer_shift[None],
+        down_weight,
+        down_bias[None],
+    )
     vmem = pl.BlockSpec(memory_space=pltpu.VMEM)
     hbm = pl.BlockSpec(memory_space=pl.ANY)
     out = pl.pallas_call(
         functools.partial(kernel, sizes),
         out_shape=jax.ShapeDtypeStruct((out_rows, chan_out), BF16),
-        in_specs=[vmem] * 9 + [hbm] * 2,
+        in_specs=[hbm] * len(operands),
         out_specs=vmem,
-        scratch_shapes=[
+        scratch_shapes=[pltpu.VMEM(operand.shape, operand.dtype) for operand in operands]
+        + [
             pltpu.VMEM((clip_n, clips * frame_n * chan, cells), BF16),
             pltpu.VMEM((clip_n, 2, clips * frame_n * chan, cells + 2 * HALO * COLS), BF16),
             pltpu.VMEM((clips, out_cells, ext_f * chan_mid), F32),
             pltpu.VMEM((clips, ext_f, out_cells, TAPS * chan_mid), BF16),
             pltpu.VMEM((clips, frame_n, cells, chan_out), F32),
-            pltpu.VMEM(mixer_flat.shape, BF16),
-            pltpu.VMEM(down_weight.shape, BF16),
             pltpu.VMEM((rounds, peers, 2 * per_round, chan_mid), F32),
             pltpu.VMEM((rounds, peers, 2 * per_round, chan_out), F32),
-            pltpu.SemaphoreType.DMA((2,)),
+            pltpu.SemaphoreType.DMA((len(operands),)),
             pltpu.SemaphoreType.DMA((clip_n, 2, 3)),
             pltpu.SemaphoreType.DMA((clip_n, 2, 3)),
             pltpu.SemaphoreType.DMA((2 * rounds, peers)),
             pltpu.SemaphoreType.DMA((2 * rounds, peers)),
         ],
         compiler_params=pltpu.CompilerParams(
-            collective_id=0, has_side_effects=True, vmem_limit_bytes=50 * 1024 * 1024
+            collective_id=0, has_side_effects=True, vmem_limit_bytes=64 * 1024 * 1024
         ),
-    )(
-        frames.reshape(slots * chan * frame_n, cells),
-        keep_list[None],
-        train_slot[None],
-        stem_weight,
-        stem_gain[None],
-        stem_shift[None],
-        mixer_gain[None],
-        mixer_shift[None],
-        down_bias[None],
-        mixer_flat,
-        down_weight,
-    )
+    )(*operands)
     return out.reshape(clips, frame_n // 2, row_n // 2, COLS // 2, chan_out)
 
 

time: 40.7 us -> 33.2 us (0.82)
  local copies, waits for them, and re-layouts: 9.42 us -> 1.67 us
  Pallas kernels: 30.9 us -> 31.4 us
    unnamed x21 -> x1, local copies, waits for them, and re-layouts: 8.6 us -> 1.67 us
    reshape x1 -> x0, local copies, waits for them, and re-layouts: 0.81 us -> none  [local(): frames.reshape(slots * chan * frame_n, cells)]
    pallas_call x1, Pallas kernels: 30.9 us -> 31.4 us  [local(): pl.pallas_call(functools.partial(kernel, sizes), out_shape=jax.ShapeDtype...]
where the time goes in v2:
time: 33.2 us; the launch traced here: 33.1 us
  Pallas kernels  31.4 us (95%)
  local copies, waits for them, and re-layouts  1.67 us (5%)
    pallas_call x1, Pallas kernels, local(): pl.pallas_call(functools.partial(kernel, sizes), out_shape=jax.ShapeDtype...  31.4 us
    unnamed x1, local copies, waits for them, and re-layouts  1.67 us

profile of v2, /device:TPU:0, one launch (start us, length us, event | category | flops | bytes accessed | tf_op | source)
XLA Modules:
  0.0 33.1 jit_solution(869116860652680943)
XLA Ops:
  0.0 31.4 %shard_map.109 = bf16[512,256]{1,0:T(8,128)(2,1)} custom-call(bf16[8,3,4,256]{3,2,1,0:T(4,128)(2,1)} %frames_hbm.1, s32[1,8]{1,0:T(1,128)} %bitcast.14, s32[1,8]{1,0:T(1,128)} %bitcast.15, bf16[81,128]{1,0:T(8,128)(2,1)} %stem_w_hbm.1, f32[1,128]{1,0:T(1,128)} %bitcast.16, f32[1,128]{1,0:T(1,128)} %bitcast.17, bf16[3456,256]{1,0:T(8,128)(2,1)} %bitcast.9, ...), custom_call_target="tpu_custom_call" | custom-call | tf_op jit(solution)/shard_map/pallas_call | solution.py:495
  31.4 1.7 %copy.13 = bf16[4,2,2,32,256]{4,3,2,1,0:T(8,128)(2,1)} copy(bf16[4,2,2,32,256]{4,3,2,1,0:T(8,128)(2,1)} %bitcast.10) | data formatting | bytes 524288

commit v3 on v2

--- a/solution.py
+++ b/solution.py
@@ -73,15 +73,14 @@
     stem_scr,
     hidden_scr,
     mixer_scr,
-    sums1,
-    sums2,
     load_sem,
     frame_send,
     frame_recv,
     sum_send,
     sum_recv,
+    *sums,
 ):
-    clip_n, row_dev, time_dev, clips, chan, frame_n, row_n, rounds = sizes
+    clip_n, row_dev, time_dev, clips, chan, frame_n, row_n, rounds1, rounds2 = sizes
     cells = row_n * COLS
     c = lax.axis_index("clip")
     r = lax.axis_index("row")
@@ -250,6 +249,13 @@
     before = jnp.where(t > 0, half_rows + base + frame_at * chan, base)
     goal = jnp.where(frame_at >= frame_n, base + (frame_at - frame_n) * chan, before)
     order = one_hot(goal == iota((total_rows, total_rows), 1))
+
+    def group_table(chan_n):
+        per_group = chan_n // GROUPS
+        group_at = quot(iota((chan_n, chan_n), 0), per_group)
+        return one_hot(group_at == quot(iota((chan_n, chan_n), 1), per_group))
+
+    joined_mid, joined_out = group_table(chan_mid), group_table(chan_out)
 
     each_move(-1, lambda copy: copy.wait_recv())
 
@@ -285,49 +291,51 @@
                 views.append(by_tap[tap][:, row_tap * COLS : row_tap * COLS + out_cells])
     filler = jnp.zeros((depth - TAPS * TAPS * lines, out_cells), F32)
 
-    def sum_copy(buffer, number, index, j):
+    def sum_copy(number, j):
         other = lax.rem(me + j, peers)
         return pltpu.make_async_remote_copy(
-            src_ref=buffer.at[index, me],
-            dst_ref=buffer.at[index, me],
-            send_sem=sum_send.at[number, j],
-            recv_sem=sum_recv.at[number, j],
+            src_ref=sums[number].at[0],
+            dst_ref=sums[number].at[j],
+            send_sem=sum_send.at[number],
+            recv_sem=sum_recv.at[number],
             device_id={"row": other // time_dev, "tm": lax.rem(other, time_dev)},
             device_id_type=MESH,
         )
 
-    def send_sums(buffer, number, index):
+    def sum_wait(number, semaphore):
+        others = sums[number].at[pl.ds(1, peers - 1)]
+        pltpu.make_async_copy(others, others, semaphore.at[number]).wait()
+
+    def send_sums(number, clip_sums):
+        for place, (value_sum, square_sum) in enumerate(clip_sums):
+            low = len(clip_sums) + place
+            sums[number][0, place : place + 1, :] = value_sum
+            sums[number][0, low : low + 1, :] = square_sum
         for j in range(1, peers):
-            sum_copy(buffer, number, index, j).start()
-
-    def take_sums(buffer, number, index, gain, shift):
+            sum_copy(number, j).start()
+
+    def take_sums(number, joined, gain, shift):
+        sum_wait(number, sum_recv)
+        total = sums[number][0]
         for j in range(1, peers):
-            sum_copy(buffer, number, index, j).wait_recv()
-        total = buffer[index, 0]
-        for j in range(1, peers):
-            total = total + buffer[index, j]
-        chan_n = total.shape[1]
-        per_group = chan_n // GROUPS
-        joined = jnp.where(
-            quot(iota((chan_n, chan_n), 0), per_group) == quot(iota((chan_n, chan_n), 1), per_group),
-            1.0,
-            0.0,
-        )
-        total = jnp.dot(
-            total, joined, preferred_element_type=F32, precision=lax.Precision.HIGHEST
-        )
-        count = peers * frame_n * cells * per_group
-        total = total * (1.0 / count)
-        half = total.shape[0] // 2
-        mean = total[:half]
-        inverse = lax.rsqrt(total[half:] - mean * mean + eps)
+            total = total + sums[number][j]
+        rows = total.shape[0]
+        high = total.astype(BF16).astype(F32)
+        middle = (total - high).astype(BF16).astype(F32)
+        low = total - high - middle
+        joint = dot(jnp.concatenate([high, middle, low], axis=0).astype(BF16), joined)
+        total = joint[:rows] + joint[rows : 2 * rows] + joint[2 * rows :]
+        per_group = total.shape[1] // GROUPS
+        total = total * (1.0 / (peers * frame_n * cells * per_group))
+        mean = total[: rows // 2]
+        inverse = lax.rsqrt(total[rows // 2 :] - mean * mean + eps)
         scale = inverse * gain
-        return scale, shift - mean * scale
-
-    per_round = clips // rounds
-    for turn in range(rounds):
-        for pos in range(per_round):
-            k = turn * per_round + pos
+        move = shift - mean * scale
+        return [(scale[i : i + 1], move[i : i + 1]) for i in range(rows // 2)]
+
+    for number, group in enumerate(rounds1):
+        clip_sums = []
+        for k in group:
             patches = jnp.concatenate(
                 [view[k * lines : (k + 1) * lines] for view in views] + [filler], axis=0
             ).astype(BF16)
@@ -343,9 +351,8 @@
             for f in range(1, frame_n):
                 value_sum = value_sum + values[:, f * chan_mid : (f + 1) * chan_mid]
                 square_sum = square_sum + squares[:, f * chan_mid : (f + 1) * chan_mid]
-            sums1[turn, me, pos : pos + 1, :] = value_sum
-            sums1[turn, me, per_round + pos : per_round + pos + 1, :] = square_sum
-        send_sums(sums1, turn, turn)
+            clip_sums.append((value_sum, square_sum))
+        send_sums(number, clip_sums)
 
     top = jnp.where(r > 0, 1.0, 0.0).astype(F32)
     bottom = jnp.where(r < row_dev - 1, 1.0, 0.0).astype(F32)
@@ -353,8 +360,8 @@
     half_cols = COLS // 2
     x_at = iota((ext_rows * half_cols, chan_mid), 0) & (half_cols - 1)
 
-    def norm_first(k, scale, shift):
-        for f in range(ext_f):
+    def norm_first(k, frames_at, scale, shift):
+        for f in frames_at:
             value = stem_scr[k, :, f * chan_mid : (f + 1) * chan_mid]
             value = silu(value * scale + shift)
             value = jnp.concatenate(
@@ -380,11 +387,11 @@
             hidden_scr[k, f, :, chan_mid : 2 * chan_mid] = value.astype(BF16)
             hidden_scr[k, f, :, 2 * chan_mid :] = after.astype(BF16)
 
-    def mix(k, turn, pos):
+    def mix(k, first, count):
         strip = jnp.concatenate(
             [
-                hidden_scr[k, a : a + frame_n, b * COLS : b * COLS + cells, :].reshape(
-                    frame_n * cells, TAPS * chan_mid
+                hidden_scr[k, first + a : first + a + count, b * COLS : b * COLS + cells, :].reshape(
+                    count * cells, TAPS * chan_mid
                 )
                 for a in range(TAPS)
                 for b in range(TAPS)
@@ -392,38 +399,51 @@
             axis=1,
         )
         mixed = dot(strip, mixer_w[...])
-        mixer_scr[k] = mixed.reshape(frame_n, cells, chan_out)
-        value_sum = jnp.sum(mixed, axis=0, keepdims=True)
-        square_sum = jnp.sum(mixed * mixed, axis=0, keepdims=True)
-        sums2[turn, me, pos : pos + 1, :] = value_sum
-        sums2[turn, me, per_round + pos : per_round + pos + 1, :] = square_sum
+        mixer_scr[k, first : first + count] = mixed.reshape(count, cells, chan_out)
+        return (
+            jnp.sum(mixed, axis=0, keepdims=True),
+            jnp.sum(mixed * mixed, axis=0, keepdims=True),
+        )
 
     for load in loads[4:7]:
         load.wait()
-    for turn in range(rounds):
-        scale, shift = take_sums(sums1, turn, turn, stem_gain_ref[...], stem_shift_ref[...])
-        for pos in range(per_round):
-            k = turn * per_round + pos
-            norm_first(k, scale[pos : pos + 1], shift[pos : pos + 1])
-            mix(k, turn, pos)
-        send_sums(sums2, rounds + turn, turn)
+    norms = {}
+
+    def take_first(number):
+        taken = take_sums(number, joined_mid, stem_gain_ref[...], stem_shift_ref[...])
+        norms.update(zip(rounds1[number], taken))
+
+    take_first(0)
+    norm_first(0, range(ext_f), *norms[0])
+    half = frame_n // 2
+    done = []
+    for k in range(clips):
+        low_sums = mix(k, 0, half)
+        if k + 1 < clips:
+            if k + 1 not in norms:
+                take_first(1)
+            norm_first(k + 1, range(ext_f), *norms[k + 1])
+        high_sums = mix(k, half, frame_n - half)
+        done.append((low_sums[0] + high_sums[0], low_sums[1] + high_sums[1]))
+        for number, group in enumerate(rounds2):
+            if group[-1] == k:
+                send_sums(len(rounds1) + number, [done[i] for i in group])
 
     for load in loads[7:]:
         load.wait()
     bias = down_bias_ref[...]
     pairs = frame_n // 2
     out_rows = row_n // 2
-    for turn in range(rounds):
-        scale, shift = take_sums(
-            sums2, rounds + turn, turn, mixer_gain_ref[...], mixer_shift_ref[...]
-        )
-        for pos in range(per_round):
-            k = turn * per_round + pos
+    for number, group in enumerate(rounds2):
+        taken = take_sums(
+            len(rounds1) + number, joined_out, mixer_gain_ref[...], mixer_shift_ref[...]
+        )
+        for k, (scale, shift) in zip(group, taken):
             squares = []
             for pair in range(pairs):
                 acts = []
                 for f in (2 * pair, 2 * pair + 1):
-                    value = mixer_scr[k, f] * scale[pos : pos + 1] + shift[pos : pos + 1]
+                    value = mixer_scr[k, f] * scale + shift
                     acts.append(silu(value).astype(BF16).astype(F32))
                 pooled = ((acts[0] + acts[1]) * 0.5).astype(BF16)
                 pooled = pooled.reshape(out_rows, 2, 2, half_cols, chan_out)
@@ -443,10 +463,8 @@
             out_ref[k * size : (k + 1) * size, :] = latent.astype(BF16)
 
     each_move(1, lambda copy: copy.wait_send())
-    for turn in range(rounds):
-        for j in range(1, peers):
-            sum_copy(sums1, turn, turn, j).wait_send()
-            sum_copy(sums2, rounds + turn, turn, j).wait_send()
+    for number in range(len(sums)):
+        sum_wait(number, sum_send)
 
 
 def local(
@@ -470,12 +488,13 @@
     row_n = cells // COLS
     chan_mid = stem_weight.shape[1]
     chan_out = mixer_weight.shape[3]
-    rounds = 2 if clips % 2 == 0 else 1
-    per_round = clips // rounds
+    every = tuple(range(clips))
+    rounds1 = tuple(part for part in (every[:1], every[1:]) if part)
+    rounds2 = tuple(part for part in (every[:-1], every[-1:]) if part)
     peers = row_dev * time_dev
     ext_f = frame_n + HALO
     out_cells = cells + 2 * COLS
-    sizes = (clip_n, row_dev, time_dev, clips, chan, frame_n, row_n, rounds)
+    sizes = (clip_n, row_dev, time_dev, clips, chan, frame_n, row_n, rounds1, rounds2)
     out_rows = clips * (frame_n // 2) * (row_n // 2) * (COLS // 2)
     operands = (
         frames,
@@ -491,7 +510,7 @@
         down_bias[None],
     )
     vmem = pl.BlockSpec(memory_space=pltpu.VMEM)
-    hbm = pl.BlockSpec(memory_space=pl.ANY)
+    hbm = pl.BlockSpec(memory_space=pltpu.HBM)
     out = pl.pallas_call(
         functools.partial(kernel, sizes),
         out_shape=jax.ShapeDtypeStruct((out_rows, chan_out), BF16),
@@ -504,14 +523,14 @@
             pltpu.VMEM((clips, out_cells, ext_f * chan_mid), F32),
             pltpu.VMEM((clips, ext_f, out_cells, TAPS * chan_mid), BF16),
             pltpu.VMEM((clips, frame_n, cells, chan_out), F32),
-            pltpu.VMEM((rounds, peers, 2 * per_round, chan_mid), F32),
-            pltpu.VMEM((rounds, peers, 2 * per_round, chan_out), F32),
             pltpu.SemaphoreType.DMA((len(operands),)),
             pltpu.SemaphoreType.DMA((clip_n, 2, 3)),
             pltpu.SemaphoreType.DMA((clip_n, 2, 3)),
-            pltpu.SemaphoreType.DMA((2 * rounds, peers)),
-            pltpu.SemaphoreType.DMA((2 * rounds, peers)),
-        ],
+            pltpu.SemaphoreType.DMA((len(rounds1) + len(rounds2),)),
+            pltpu.SemaphoreType.DMA((len(rounds1) + len(rounds2),)),
+        ]
+        + [pltpu.VMEM((peers, 2 * len(part), chan_mid), F32) for part in rounds1]
+        + [pltpu.VMEM((peers, 2 * len(part), chan_out), F32) for part in rounds2],
         compiler_params=pltpu.CompilerParams(
             collective_id=0, has_side_effects=True, vmem_limit_bytes=64 * 1024 * 1024
         ),

time: 33.2 us -> 33.4 us (level)
  no operation moved by 1% of the time
where the time goes in v3:
time: 33.4 us; the launch traced here: 33.2 us
  Pallas kernels  31.6 us (95%)
  local copies, waits for them, and re-layouts  1.67 us (5%)
    pallas_call x1, Pallas kernels, local(): pl.pallas_call(functools.partial(kernel, sizes), out_shape=jax.ShapeDtype...  31.6 us
    unnamed x1, local copies, waits for them, and re-layouts  1.67 us

profile of v3, /device:TPU:0, one launch (start us, length us, event | category | flops | bytes accessed | tf_op | source)
XLA Modules:
  0.0 33.2 jit_solution(13887413282975847447)
XLA Ops:
  0.0 31.6 %shard_map.109 = bf16[512,256]{1,0:T(8,128)(2,1)} custom-call(bf16[8,3,4,256]{3,2,1,0:T(4,128)(2,1)} %frames_hbm.1, s32[1,8]{1,0:T(1,128)} %bitcast.14, s32[1,8]{1,0:T(1,128)} %bitcast.15, bf16[81,128]{1,0:T(8,128)(2,1)} %stem_w_hbm.1, f32[1,128]{1,0:T(1,128)} %bitcast.16, f32[1,128]{1,0:T(1,128)} %bitcast.17, bf16[3456,256]{1,0:T(8,128)(2,1)} %bitcast.9, ...), custom_call_target="tpu_custom_call" | custom-call | tf_op jit(solution)/shard_map/pallas_call | solution.py:514
  31.6 1.7 %copy.13 = bf16[4,2,2,32,256]{4,3,2,1,0:T(8,128)(2,1)} copy(bf16[4,2,2,32,256]{4,3,2,1,0:T(8,128)(2,1)} %bitcast.10) | data formatting | bytes 524288

commit v4 on v3

--- a/solution.py
+++ b/solution.py
@@ -73,6 +73,11 @@
     stem_scr,
     hidden_scr,
     mixer_scr,
+    view_scr,
+    own1,
+    own2,
+    norm1,
+    norm2,
     load_sem,
     frame_send,
     frame_recv,
@@ -119,7 +124,9 @@
     landed[...] = jnp.zeros_like(landed)
 
     barrier = pltpu.get_barrier_semaphore()
-    for j in range(1, peers):
+
+    @pl.loop(1, peers)
+    def _(j):
         other = lax.rem(me + j, peers)
         pl.semaphore_signal(
             barrier,
@@ -127,6 +134,7 @@
             device_id={"row": other // time_dev, "tm": lax.rem(other, time_dev)},
             device_id_type=MESH,
         )
+
     rows_near = 1 + (r > 0).astype(jnp.int32) + (r < row_dev - 1).astype(jnp.int32)
     times_near = 1 + (t > 0).astype(jnp.int32) + (t < time_dev - 1).astype(jnp.int32)
     for k in range(1, clip_n):
@@ -289,6 +297,8 @@
                 )
             else:
                 views.append(by_tap[tap][:, row_tap * COLS : row_tap * COLS + out_cells])
+    for number, view in enumerate(views):
+        view_scr[number] = view
     filler = jnp.zeros((depth - TAPS * TAPS * lines, out_cells), F32)
 
     def sum_copy(number, j):
@@ -306,15 +316,17 @@
         others = sums[number].at[pl.ds(1, peers - 1)]
         pltpu.make_async_copy(others, others, semaphore.at[number]).wait()
 
-    def send_sums(number, clip_sums):
-        for place, (value_sum, square_sum) in enumerate(clip_sums):
-            low = len(clip_sums) + place
-            sums[number][0, place : place + 1, :] = value_sum
-            sums[number][0, low : low + 1, :] = square_sum
-        for j in range(1, peers):
+    def send_sums(number, own, group):
+        for place, k in enumerate(group):
+            low = len(group) + place
+            sums[number][0, place : place + 1, :] = own[k, 0:1, :]
+            sums[number][0, low : low + 1, :] = own[k, 1:2, :]
+
+        @pl.loop(1, peers)
+        def _(j):
             sum_copy(number, j).start()
 
-    def take_sums(number, joined, gain, shift):
+    def take_sums(number, joined, gain, shift, norm, group):
         sum_wait(number, sum_recv)
         total = sums[number][0]
         for j in range(1, peers):
@@ -331,28 +343,37 @@
         inverse = lax.rsqrt(total[rows // 2 :] - mean * mean + eps)
         scale = inverse * gain
         move = shift - mean * scale
-        return [(scale[i : i + 1], move[i : i + 1]) for i in range(rows // 2)]
-
-    for number, group in enumerate(rounds1):
-        clip_sums = []
-        for k in group:
-            patches = jnp.concatenate(
-                [view[k * lines : (k + 1) * lines] for view in views] + [filler], axis=0
-            ).astype(BF16)
-            stem = lax.dot_general(
-                patches, stem_big, (((0,), (0,)), ((), ())), preferred_element_type=F32
-            )
-            stem_scr[k] = stem
-            own = stem[COLS : COLS + cells, HALO * chan_mid :]
-            values = jnp.sum(own, axis=0, keepdims=True)
-            squares = jnp.sum(own * own, axis=0, keepdims=True)
-            value_sum = values[:, :chan_mid]
-            square_sum = squares[:, :chan_mid]
-            for f in range(1, frame_n):
-                value_sum = value_sum + values[:, f * chan_mid : (f + 1) * chan_mid]
-                square_sum = square_sum + squares[:, f * chan_mid : (f + 1) * chan_mid]
-            clip_sums.append((value_sum, square_sum))
-        send_sums(number, clip_sums)
+        for place, k in enumerate(group):
+            norm[k, 0:1, :] = scale[place : place + 1]
+            norm[k, 1:2, :] = move[place : place + 1]
+
+    @pl.loop(0, clips)
+    def _(k):
+        first_line = pl.multiple_of(k * lines, 8)
+        patches = jnp.concatenate(
+            [view_scr[number, pl.ds(first_line, lines), :] for number in range(TAPS * TAPS)]
+            + [filler],
+            axis=0,
+        ).astype(BF16)
+        stem = lax.dot_general(
+            patches, stem_big, (((0,), (0,)), ((), ())), preferred_element_type=F32
+        )
+        value_sum = jnp.zeros((1, chan_mid), F32)
+        square_sum = jnp.zeros((1, chan_mid), F32)
+        for f in range(ext_f):
+            part = stem[:, f * chan_mid : (f + 1) * chan_mid]
+            stem_scr[k, f] = part
+            if f >= HALO:
+                own = part[COLS : COLS + cells]
+                value_sum = value_sum + jnp.sum(own, axis=0, keepdims=True)
+                square_sum = square_sum + jnp.sum(own * own, axis=0, keepdims=True)
+        own1[k, 0:1, :] = value_sum
+        own1[k, 1:2, :] = square_sum
+        for number, group in enumerate(rounds1):
+
+            @pl.when(k == group[-1])
+            def _():
+                send_sums(number, own1, group)
 
     top = jnp.where(r > 0, 1.0, 0.0).astype(F32)
     bottom = jnp.where(r < row_dev - 1, 1.0, 0.0).astype(F32)
@@ -360,9 +381,10 @@
     half_cols = COLS // 2
     x_at = iota((ext_rows * half_cols, chan_mid), 0) & (half_cols - 1)
 
-    def norm_first(k, frames_at, scale, shift):
+    def norm_first(k, frames_at):
+        scale, shift = norm1[k, 0:1, :], norm1[k, 1:2, :]
         for f in frames_at:
-            value = stem_scr[k, :, f * chan_mid : (f + 1) * chan_mid]
+            value = stem_scr[k, f]
             value = silu(value * scale + shift)
             value = jnp.concatenate(
                 [
@@ -390,16 +412,16 @@
     def mix(k, first, count):
         strip = jnp.concatenate(
             [
-                hidden_scr[k, first + a : first + a + count, b * COLS : b * COLS + cells, :].reshape(
-                    count * cells, TAPS * chan_mid
-                )
+                hidden_scr[
+                    k, pl.ds(first + a, count), b * COLS : b * COLS + cells, :
+                ].reshape(count * cells, TAPS * chan_mid)
                 for a in range(TAPS)
                 for b in range(TAPS)
             ],
             axis=1,
         )
         mixed = dot(strip, mixer_w[...])
-        mixer_scr[k, first : first + count] = mixed.reshape(count, cells, chan_out)
+        mixer_scr[k, pl.ds(first, count)] = mixed.reshape(count, cells, chan_out)
         return (
             jnp.sum(mixed, axis=0, keepdims=True),
             jnp.sum(mixed * mixed, axis=0, keepdims=True),
@@ -407,60 +429,80 @@
 
     for load in loads[4:7]:
         load.wait()
-    norms = {}
-
-    def take_first(number):
-        taken = take_sums(number, joined_mid, stem_gain_ref[...], stem_shift_ref[...])
-        norms.update(zip(rounds1[number], taken))
-
-    take_first(0)
-    norm_first(0, range(ext_f), *norms[0])
-    half = frame_n // 2
-    done = []
-    for k in range(clips):
-        low_sums = mix(k, 0, half)
-        if k + 1 < clips:
-            if k + 1 not in norms:
-                take_first(1)
-            norm_first(k + 1, range(ext_f), *norms[k + 1])
-        high_sums = mix(k, half, frame_n - half)
-        done.append((low_sums[0] + high_sums[0], low_sums[1] + high_sums[1]))
+    step = frame_n // 2
+
+    @pl.loop(0, clips)
+    def _(k):
+        for number, group in enumerate(rounds1):
+
+            @pl.when(k == group[0])
+            def _():
+                take_sums(
+                    number, joined_mid, stem_gain_ref[...], stem_shift_ref[...], norm1, group
+                )
+
+        @pl.loop(0, ext_f // 2)
+        def _(f):
+            norm_first(k, (2 * f, 2 * f + 1))
+
+        def mix_step(i, so_far):
+            value_sum, square_sum = mix(k, i * step, step)
+            return so_far[0] + value_sum, so_far[1] + square_sum
+
+        nothing = jnp.zeros((1, chan_out), F32)
+        value_sum, square_sum = lax.fori_loop(0, frame_n // step, mix_step, (nothing, nothing))
+        own2[k, 0:1, :] = value_sum
+        own2[k, 1:2, :] = square_sum
         for number, group in enumerate(rounds2):
-            if group[-1] == k:
-                send_sums(len(rounds1) + number, [done[i] for i in group])
+
+            @pl.when(k == group[-1])
+            def _():
+                send_sums(len(rounds1) + number, own2, group)
 
     for load in loads[7:]:
         load.wait()
     bias = down_bias_ref[...]
     pairs = frame_n // 2
     out_rows = row_n // 2
-    for number, group in enumerate(rounds2):
-        taken = take_sums(
-            len(rounds1) + number, joined_out, mixer_gain_ref[...], mixer_shift_ref[...]
-        )
-        for k, (scale, shift) in zip(group, taken):
-            squares = []
-            for pair in range(pairs):
-                acts = []
-                for f in (2 * pair, 2 * pair + 1):
-                    value = mixer_scr[k, f] * scale + shift
-                    acts.append(silu(value).astype(BF16).astype(F32))
-                pooled = ((acts[0] + acts[1]) * 0.5).astype(BF16)
-                pooled = pooled.reshape(out_rows, 2, 2, half_cols, chan_out)
-                squares.append(
-                    jnp.concatenate(
-                        [
-                            pooled[:, p, q].reshape(out_rows * half_cols, chan_out)
-                            for p in range(2)
-                            for q in range(2)
-                        ],
-                        axis=1,
-                    )
+    size = pairs * out_rows * half_cols
+
+    @pl.loop(0, clips)
+    def _(k):
+        for number, group in enumerate(rounds2):
+
+            @pl.when(k == group[0])
+            def _():
+                take_sums(
+                    len(rounds1) + number,
+                    joined_out,
+                    mixer_gain_ref[...],
+                    mixer_shift_ref[...],
+                    norm2,
+                    group,
                 )
-            block = jnp.concatenate(squares, axis=0)
-            latent = dot(block, down_w[...]) + bias
-            size = block.shape[0]
-            out_ref[k * size : (k + 1) * size, :] = latent.astype(BF16)
+
+        scale, shift = norm2[k, 0:1, :], norm2[k, 1:2, :]
+        squares = []
+        for pair in range(pairs):
+            acts = []
+            for f in (2 * pair, 2 * pair + 1):
+                value = mixer_scr[k, f] * scale + shift
+                acts.append(silu(value).astype(BF16).astype(F32))
+            pooled = ((acts[0] + acts[1]) * 0.5).astype(BF16)
+            pooled = pooled.reshape(out_rows, 2, 2, half_cols, chan_out)
+            squares.append(
+                jnp.concatenate(
+                    [
+                        pooled[:, p, q].reshape(out_rows * half_cols, chan_out)
+                        for p in range(2)
+                        for q in range(2)
+                    ],
+                    axis=1,
+                )
+            )
+        block = jnp.concatenate(squares, axis=0)
+        latent = dot(block, down_w[...]) + bias
+        out_ref[pl.ds(pl.multiple_of(k * size, size), size), :] = latent.astype(BF16)
 
     each_move(1, lambda copy: copy.wait_send())
     for number in range(len(sums)):
@@ -520,9 +562,14 @@
         + [
             pltpu.VMEM((clip_n, clips * frame_n * chan, cells), BF16),
             pltpu.VMEM((clip_n, 2, clips * frame_n * chan, cells + 2 * HALO * COLS), BF16),
-            pltpu.VMEM((clips, out_cells, ext_f * chan_mid), F32),
+            pltpu.VMEM((clips, ext_f, out_cells, chan_mid), F32),
             pltpu.VMEM((clips, ext_f, out_cells, TAPS * chan_mid), BF16),
             pltpu.VMEM((clips, frame_n, cells, chan_out), F32),
+            pltpu.VMEM((TAPS * TAPS, 2 * clips * frame_n * chan, out_cells), F32),
+            pltpu.VMEM((clips, 2, chan_mid), F32),
+            pltpu.VMEM((clips, 2, chan_out), F32),
+            pltpu.VMEM((clips, 2, chan_mid), F32),
+            pltpu.VMEM((clips, 2, chan_out), F32),
             pltpu.SemaphoreType.DMA((len(operands),)),
             pltpu.SemaphoreType.DMA((clip_n, 2, 3)),
             pltpu.SemaphoreType.DMA((clip_n, 2, 3)),

time: 33.4 us -> 34.2 us (1.024)
  Pallas kernels: 31.6 us -> 32.4 us
    pallas_call x1, Pallas kernels: 31.6 us -> 32.4 us  [local(): pl.pallas_call(functools.partial(kernel, sizes), out_shape=jax.ShapeDtype...]
where the time goes in v4:
time: 34.2 us; the launch traced here: 34.1 us
  Pallas kernels  32.4 us (95%)
  local copies, waits for them, and re-layouts  1.67 us (5%)
    pallas_call x1, Pallas kernels, local(): pl.pallas_call(functools.partial(kernel, sizes), out_shape=jax.ShapeDtype...  32.4 us
    unnamed x1, local copies, waits for them, and re-layouts  1.67 us

profile of v4, /device:TPU:0, one launch (start us, length us, event | category | flops | bytes accessed | tf_op | source)
XLA Modules:
  0.0 34.1 jit_solution(6828267331081753158)
XLA Ops:
  0.0 32.4 %shard_map.109 = bf16[512,256]{1,0:T(8,128)(2,1)} custom-call(bf16[8,3,4,256]{3,2,1,0:T(4,128)(2,1)} %frames_hbm.1, s32[1,8]{1,0:T(1,128)} %bitcast.14, s32[1,8]{1,0:T(1,128)} %bitcast.15, bf16[81,128]{1,0:T(8,128)(2,1)} %stem_w_hbm.1, f32[1,128]{1,0:T(1,128)} %bitcast.16, f32[1,128]{1,0:T(1,128)} %bitcast.17, bf16[3456,256]{1,0:T(8,128)(2,1)} %bitcast.9, ...), custom_call_target="tpu_custom_call" | custom-call | tf_op jit(solution)/shard_map/pallas_call | solution.py:556
  32.4 1.7 %copy.13 = bf16[4,2,2,32,256]{4,3,2,1,0:T(8,128)(2,1)} copy(bf16[4,2,2,32,256]{4,3,2,1,0:T(8,128)(2,1)} %bitcast.10) | data formatting | bytes 524288

commit v5 on v3

--- a/solution.py
+++ b/solution.py
@@ -532,9 +532,9 @@
         + [pltpu.VMEM((peers, 2 * len(part), chan_mid), F32) for part in rounds1]
         + [pltpu.VMEM((peers, 2 * len(part), chan_out), F32) for part in rounds2],
         compiler_params=pltpu.CompilerParams(
-            collective_id=0, has_side_effects=True, vmem_limit_bytes=64 * 1024 * 1024
+            collective_id=0, has_side_effects=True, vmem_limit_bytes=50 * 1024 * 1024
         ),
-    )(*operands)
+    )(*(pltpu.with_memory_space_constraint(operand, pltpu.HBM) for operand in operands))
     return out.reshape(clips, frame_n // 2, row_n // 2, COLS // 2, chan_out)
 
 

time: 33.4 us -> 31.7 us (0.949)
  local copies, waits for them, and re-layouts: 1.67 us -> 0.71 us
  Pallas kernels: 31.6 us -> 30.9 us
    unnamed x1, local copies, waits for them, and re-layouts: 1.67 us -> 0.71 us
    pallas_call x1, Pallas kernels: 31.6 us -> 30.9 us  [local(): pl.pallas_call(functools.partial(kernel, sizes), out_shape=jax.ShapeDtype...]
where the time goes in v5:
time: 31.7 us; the launch traced here: 31.6 us
  Pallas kernels  30.9 us (97%)
  local copies, waits for them, and re-layouts  0.71 us (2%)
    pallas_call x1, Pallas kernels, local(): pl.pallas_call(functools.partial(kernel, sizes), out_shape=jax.ShapeDtype...  30.9 us
    unnamed x1, local copies, waits for them, and re-layouts  0.71 us

profile of v5, /device:TPU:0, one launch (start us, length us, event | category | flops | bytes accessed | tf_op | source)
XLA Modules:
  0.0 31.6 jit_solution(7194180138515119306)
XLA Ops:
  0.0 30.9 %shard_map.109 = bf16[512,256]{1,0:T(8,128)(2,1)S(1)} custom-call(bf16[8,3,4,256]{3,2,1,0:T(4,128)(2,1)} %frames_hbm.1, s32[1,8]{1,0:T(1,128)} %bitcast.14, s32[1,8]{1,0:T(1,128)} %bitcast.15, bf16[81,128]{1,0:T(8,128)(2,1)} %stem_w_hbm.1, f32[1,128]{1,0:T(1,128)} %bitcast.16, f32[1,128]{1,0:T(1,128)} %bitcast.17, bf16[3456,256]{1,0:T(8,128)(2,1)} %bitcast.10, ...), custom_call_target="tpu_custom_call" | custom-call | tf_op jit(solution)/shard_map/pallas_call | solution.py:514
  30.9 0.7 %copy.13 = bf16[4,2,2,32,256]{4,3,2,1,0:T(8,128)(2,1)} copy(bf16[4,2,2,32,256]{4,3,2,1,0:T(8,128)(2,1)S(1)} %bitcast.9) | data formatting | bytes 524288

commit v6 on v5

--- a/solution.py
+++ b/solution.py
@@ -85,7 +85,8 @@
     c = lax.axis_index("clip")
     r = lax.axis_index("row")
     t = lax.axis_index("tm")
-    me = r * time_dev + t
+    rows_at = [jnp.where(r + j < row_dev, r + j, r + j - row_dev) for j in range(row_dev)]
+    times_at = [jnp.where(t + j < time_dev, t + j, t + j - time_dev) for j in range(time_dev)]
     peers = row_dev * time_dev
     per_clip = frame_n * chan
     halo_cells = HALO * COLS
@@ -120,11 +121,10 @@
 
     barrier = pltpu.get_barrier_semaphore()
     for j in range(1, peers):
-        other = lax.rem(me + j, peers)
         pl.semaphore_signal(
             barrier,
             inc=1,
-            device_id={"row": other // time_dev, "tm": lax.rem(other, time_dev)},
+            device_id={"row": rows_at[j // time_dev], "tm": times_at[j % time_dev]},
             device_id_type=MESH,
         )
     rows_near = 1 + (r > 0).astype(jnp.int32) + (r < row_dev - 1).astype(jnp.int32)
@@ -292,13 +292,12 @@
     filler = jnp.zeros((depth - TAPS * TAPS * lines, out_cells), F32)
 
     def sum_copy(number, j):
-        other = lax.rem(me + j, peers)
         return pltpu.make_async_remote_copy(
             src_ref=sums[number].at[0],
             dst_ref=sums[number].at[j],
             send_sem=sum_send.at[number],
             recv_sem=sum_recv.at[number],
-            device_id={"row": other // time_dev, "tm": lax.rem(other, time_dev)},
+            device_id={"row": rows_at[j // time_dev], "tm": times_at[j % time_dev]},
             device_id_type=MESH,
         )
 
@@ -414,11 +413,13 @@
         norms.update(zip(rounds1[number], taken))
 
     take_first(0)
-    norm_first(0, range(ext_f), *norms[0])
     half = frame_n // 2
+    norm_first(0, range(half + HALO), *norms[0])
     done = []
     for k in range(clips):
         low_sums = mix(k, 0, half)
+        if k == 0:
+            norm_first(0, range(half + HALO, ext_f), *norms[0])
         if k + 1 < clips:
             if k + 1 not in norms:
                 take_first(1)

time: 31.7 us -> 31.7 us (level)
  no operation moved by 1% of the time
where the time goes in v6:
time: 31.7 us; the launch traced here: 31.6 us
  Pallas kernels  30.9 us (97%)
  local copies, waits for them, and re-layouts  0.71 us (2%)
    pallas_call x1, Pallas kernels, local(): pl.pallas_call(functools.partial(kernel, sizes), out_shape=jax.ShapeDtype...  30.9 us
    unnamed x1, local copies, waits for them, and re-layouts  0.71 us

profile of v6, /device:TPU:0, one launch (start us, length us, event | category | flops | bytes accessed | tf_op | source)
XLA Modules:
  0.0 31.6 jit_solution(10886088594209608379)
XLA Ops:
  0.0 30.9 %shard_map.109 = bf16[512,256]{1,0:T(8,128)(2,1)S(1)} custom-call(bf16[8,3,4,256]{3,2,1,0:T(4,128)(2,1)} %frames_hbm.1, s32[1,8]{1,0:T(1,128)} %bitcast.14, s32[1,8]{1,0:T(1,128)} %bitcast.15, bf16[81,128]{1,0:T(8,128)(2,1)} %stem_w_hbm.1, f32[1,128]{1,0:T(1,128)} %bitcast.16, f32[1,128]{1,0:T(1,128)} %bitcast.17, bf16[3456,256]{1,0:T(8,128)(2,1)} %bitcast.10, ...), custom_call_target="tpu_custom_call" | custom-call | tf_op jit(solution)/shard_map/pallas_call | solution.py:515
  30.9 0.7 %copy.13 = bf16[4,2,2,32,256]{4,3,2,1,0:T(8,128)(2,1)} copy(bf16[4,2,2,32,256]{4,3,2,1,0:T(8,128)(2,1)S(1)} %bitcast.9) | data formatting | bytes 524288

commit v7 on v6

--- a/solution.py
+++ b/solution.py
@@ -413,19 +413,20 @@
         norms.update(zip(rounds1[number], taken))
 
     take_first(0)
-    half = frame_n // 2
-    norm_first(0, range(half + HALO), *norms[0])
     done = []
+    norm_first(0, range(TAPS), *norms[0])
     for k in range(clips):
-        low_sums = mix(k, 0, half)
-        if k == 0:
-            norm_first(0, range(half + HALO, ext_f), *norms[0])
-        if k + 1 < clips:
-            if k + 1 not in norms:
-                take_first(1)
-            norm_first(k + 1, range(ext_f), *norms[k + 1])
-        high_sums = mix(k, half, frame_n - half)
-        done.append((low_sums[0] + high_sums[0], low_sums[1] + high_sums[1]))
+        parts = []
+        for f in range(frame_n):
+            parts.append(mix(k, f, 1))
+            if k == 0 and f + TAPS < ext_f:
+                norm_first(0, (f + TAPS,), *norms[0])
+            if k + 1 < clips and f > 0:
+                if k + 1 not in norms:
+                    take_first(1)
+                low = (f - 1) * ext_f // (frame_n - 1)
+                norm_first(k + 1, range(low, f * ext_f // (frame_n - 1)), *norms[k + 1])
+        done.append((sum(part[0] for part in parts), sum(part[1] for part in parts)))
         for number, group in enumerate(rounds2):
             if group[-1] == k:
                 send_sums(len(rounds1) + number, [done[i] for i in group])

time: 31.7 us -> 30 us (0.946)
  Pallas kernels: 30.9 us -> 29.1 us
    pallas_call x1, Pallas kernels: 30.9 us -> 29.1 us  [local(): pl.pallas_call(functools.partial(kernel, sizes), out_shape=jax.ShapeDtype...]
where the time goes in v7:
time: 30 us; the launch traced here: 29.8 us
  Pallas kernels  29.1 us (97%)
  local copies, waits for them, and re-layouts  0.71 us (2%)
    pallas_call x1, Pallas kernels, local(): pl.pallas_call(functools.partial(kernel, sizes), out_shape=jax.ShapeDtype...  29.1 us
    unnamed x1, local copies, waits for them, and re-layouts  0.71 us

profile of v7, /device:TPU:0, one launch (start us, length us, event | category | flops | bytes accessed | tf_op | source)
XLA Modules:
  0.0 29.8 jit_solution(16646931326600961248)
XLA Ops:
  0.0 29.1 %shard_map.109 = bf16[512,256]{1,0:T(8,128)(2,1)S(1)} custom-call(bf16[8,3,4,256]{3,2,1,0:T(4,128)(2,1)} %frames_hbm.1, s32[1,8]{1,0:T(1,128)} %bitcast.14, s32[1,8]{1,0:T(1,128)} %bitcast.15, bf16[81,128]{1,0:T(8,128)(2,1)} %stem_w_hbm.1, f32[1,128]{1,0:T(1,128)} %bitcast.16, f32[1,128]{1,0:T(1,128)} %bitcast.17, bf16[3456,256]{1,0:T(8,128)(2,1)} %bitcast.10, ...), custom_call_target="tpu_custom_call" | custom-call | tf_op jit(solution)/shard_map/pallas_call | solution.py:516
  29.1 0.7 %copy.13 = bf16[4,2,2,32,256]{4,3,2,1,0:T(8,128)(2,1)} copy(bf16[4,2,2,32,256]{4,3,2,1,0:T(8,128)(2,1)S(1)} %bitcast.9) | data formatting | bytes 524288
